TPU v7x, 32 devices: a whole 2x2x4 slice. The times are simulated.
32 devices in a mesh: dir: 2 (over core), rows: 16 (over z, y, x).
Axes of the slice: x: 2, y: 2, z: 4, core: 2. Of those that a mesh axis runs over, the one named last changes fastest.
Arguments:
- spectra: bfloat16 [16, 64, 2, 41, 128], P('rows', None, 'dir'), may hold values from -6 to 6
- mask_grad: bfloat16 [16, 64, 2, 41, 128], P('rows', None, 'dir'), may hold values from -6 to 6
- clip_starts: int32 [16, 64, 2], P('rows'), may hold values from 0 to 1, as said below
- split_weight: float32 [5248, 128], P('rows'), may hold values from -0.5 to 0.5
- split_velocity: float32 [5248, 128], P('rows'), may hold values from -0.009765625 to 0.009765625
- split_average: float32 [5248, 128], P('rows'), may hold values from -0.5 to 0.5
- lstm_weight: float32 [1536, 1024], P('rows'), may hold values from -0.3125 to 0.3125
- lstm_velocity: float32 [1536, 1024], P('rows'), may hold values from -0.009765625 to 0.009765625
- lstm_average: float32 [1536, 1024], P('rows'), may hold values from -0.3125 to 0.3125
- proj_weight: float32 [1024, 128], P('rows'), may hold values from -0.5 to 0.5
- proj_velocity: float32 [1024, 128], P('rows'), may hold values from -0.009765625 to 0.009765625
- proj_average: float32 [1024, 128], P('rows'), may hold values from -0.5 to 0.5
- up_weight: float32 [5248, 512], P('rows'), may hold values from -0.5 to 0.5
- up_velocity: float32 [5248, 512], P('rows'), may hold values from -0.009765625 to 0.009765625
- up_average: float32 [5248, 512], P('rows'), may hold values from -0.5 to 0.5
- down_weight: float32 [20992, 256], P('rows'), may hold values from -0.25 to 0.25
- down_velocity: float32 [20992, 256], P('rows'), may hold values from -0.009765625 to 0.009765625
- down_average: float32 [20992, 256], P('rows'), may hold values from -0.25 to 0.25
- gain_weight: float32 [84, 128], replicated, may hold values from 0.5 to 1.5
- gain_velocity: float32 [84, 128], replicated, may hold values from -0.009765625 to 0.009765625
- gain_average: float32 [84, 128], replicated, may hold values from 0.1 to 1.9
- bias_weight: float32 [321, 128], replicated, may hold values from -3 to 7
- bias_velocity: float32 [321, 128], replicated, may hold values from -0.009765625 to 0.009765625
- bias_average: float32 [321, 128], replicated, may hold values from -1.2 to 1.2
Outputs:
- band_mask: bfloat16 [16, 64, 2, 41, 128], P('rows', None, 'dir')
- spectra_grad: float32 [16, 64, 2, 41, 128], P('rows', None, 'dir')
- grad_norm: float32 [], replicated
- split_grad: float32 [5248, 128], P('rows')
- split_velocity_new: float32 [5248, 128], P('rows')
- split_weight_new: float32 [5248, 128], P('rows')
- split_average_new: float32 [5248, 128], P('rows')
- lstm_grad: float32 [1536, 1024], P('rows')
- lstm_velocity_new: float32 [1536, 1024], P('rows')
- lstm_weight_new: float32 [1536, 1024], P('rows')
- lstm_average_new: float32 [1536, 1024], P('rows')
- proj_grad: float32 [1024, 128], P('rows')
- proj_velocity_new: float32 [1024, 128], P('rows')
- proj_weight_new: float32 [1024, 128], P('rows')
- proj_average_new: float32 [1024, 128], P('rows')
- up_grad: float32 [5248, 512], P('rows')
- up_velocity_new: float32 [5248, 512], P('rows')
- up_weight_new: float32 [5248, 512], P('rows')
- up_average_new: float32 [5248, 512], P('rows')
- down_grad: float32 [20992, 256], P('rows')
- down_velocity_new: float32 [20992, 256], P('rows')
- down_weight_new: float32 [20992, 256], P('rows')
- down_average_new: float32 [20992, 256], P('rows')
- gain_grad: float32 [84, 128], replicated
- gain_velocity_new: float32 [84, 128], replicated
- gain_weight_new: float32 [84, 128], replicated
- gain_average_new: float32 [84, 128], replicated
- bias_grad: float32 [321, 128], replicated
- bias_velocity_new: float32 [321, 128], replicated
- bias_weight_new: float32 [321, 128], replicated
- bias_average_new: float32 [321, 128], replicated
Inputs may be any that keep to these rules, and one draw needn't show every extreme that they name: `clip_starts`: each packed sequence of 256 frames has exactly one frame flagged 1, at any of its frames; all others are 0.
All inputs are finite; a program needn't handle non-finite values.
Results may differ from a plain program's by a relative error of at most 0.018.
Values may be sent and summed in bfloat16 or wider, within the bound.
No kernel may reach another device: no remote copies, remote signals or barrier semaphores. Data moves between devices by JAX's collectives and lax.ppermute only.
A program may use at most 320 MiB of HBM per device.

v0:
```python
import jax
import jax.numpy as jnp
from jax import lax
from jax.sharding import PartitionSpec as P

D = 128
H = 256
BANDS = 41
SUBF = 128
CHAIN = 4


EPSILON = 1e-05
MOMENTUM = 0.9
LEARN_RATE = 5.0
GAIN_RATE = 50.0
AVERAGE = 0.5
CLIP_NORM = 5.0


def shifted(block, axis, distance):
    devices = range(lax.axis_size(axis))
    route = [(i - distance, i) for i in devices if i - distance in devices]
    return lax.ppermute(block, axis, route)


def layer_norm(values, gain_row):
    centre = values - jnp.mean(values, axis=-1, keepdims=True)
    spread = jnp.mean(centre * centre, axis=-1, keepdims=True)
    return centre * lax.rsqrt(spread + EPSILON) * gain_row


def norm_back(values, gain_row, grad_out, sum_axes):
    centre = values - jnp.mean(values, axis=-1, keepdims=True)
    inverse = lax.rsqrt(jnp.mean(centre * centre, axis=-1, keepdims=True) + EPSILON)
    scaled = centre * inverse
    gain_grad = jnp.sum(grad_out * scaled, axis=sum_axes)
    scaled_grad = grad_out * gain_row
    inner_mean = jnp.mean(scaled_grad * scaled, axis=-1, keepdims=True)
    grad_in = inverse * (
        scaled_grad - jnp.mean(scaled_grad, axis=-1, keepdims=True) - scaled * inner_mean
    )
    return (grad_in, gain_grad)


def gate_split(gate_vals, hidden_width):
    in_gate = jax.nn.sigmoid(gate_vals[:, :hidden_width])
    forget = jax.nn.sigmoid(gate_vals[:, hidden_width : 2 * hidden_width])
    candidate = jnp.tanh(gate_vals[:, 2 * hidden_width : 3 * hidden_width])
    outlet = jax.nn.sigmoid(gate_vals[:, 3 * hidden_width :])
    return (in_gate, forget, candidate, outlet)


def run_block(gate_in, keeper, first_hidden, first_cell, recur_mat):
    hidden_width = recur_mat.shape[0]

    def advance(carried, inputs):
        hidden, cell_state = carried
        gate_step, keep_step = inputs
        keep_col = keep_step[:, None]
        kept_hidden = hidden * keep_col.astype(jnp.bfloat16)
        gate_vals = gate_step + jnp.dot(kept_hidden, recur_mat, preferred_element_type=jnp.float32)
        in_gate, forget, candidate, outlet = gate_split(gate_vals, hidden_width)
        new_cell = forget * (cell_state * keep_col) + in_gate * candidate
        new_hidden = (outlet * jnp.tanh(new_cell)).astype(jnp.bfloat16)
        return ((new_hidden, new_cell), (new_hidden, new_cell))

    (last_hidden, last_cell), (hiddens, cells) = lax.scan(
        advance, (first_hidden, first_cell), (gate_in, keeper)
    )
    return (hiddens, cells, last_hidden, last_cell)


def back_block(
    gate_in,
    keeper,
    first_hidden,
    first_cell,
    hiddens,
    cells,
    hidden_grads,
    last_hidden_grad,
    last_cell_grad,
    recur_mat,
):
    hidden_width = recur_mat.shape[0]
    prev_hidden = jnp.concatenate([first_hidden[None], hiddens[:-1]], axis=0)
    prev_cell = jnp.concatenate([first_cell[None], cells[:-1]], axis=0)

    def retreat(carried, inputs):
        hidden_grad, cell_grad = carried
        gate_step, keep_step, hidden_prev, cell_prev, cell_now, grad_out = inputs
        keep_col = keep_step[:, None]
        kept_hidden = hidden_prev * keep_col.astype(jnp.bfloat16)
        kept_cell = cell_prev * keep_col
        gate_vals = gate_step + jnp.dot(kept_hidden, recur_mat, preferred_element_type=jnp.float32)
        in_gate, forget, candidate, outlet = gate_split(gate_vals, hidden_width)
        squash = jnp.tanh(cell_now)
        total_grad = grad_out + hidden_grad
        cell_total = cell_grad + total_grad * outlet * (1.0 - squash * squash)
        gate_grad = jnp.concatenate(
            [
                cell_total * candidate * in_gate * (1.0 - in_gate),
                cell_total * kept_cell * forget * (1.0 - forget),
                cell_total * in_gate * (1.0 - candidate * candidate),
                total_grad * squash * outlet * (1.0 - outlet),
            ],
            axis=-1,
        ).astype(jnp.bfloat16)
        prev_grad = (
            jnp.einsum("ng,hg->nh", gate_grad, recur_mat, preferred_element_type=jnp.float32)
            * keep_col
        )
        prev_cell_grad = cell_total * forget * keep_col
        return ((prev_grad, prev_cell_grad), (gate_grad, kept_hidden))

    (first_hidden_grad, first_cell_grad), (gate_grads, kept_hiddens) = lax.scan(
        retreat,
        (last_hidden_grad, last_cell_grad),
        (gate_in, keeper, prev_hidden, prev_cell, cells, hidden_grads),
        reverse=True,
    )
    recur_grad = jnp.einsum(
        "tnh,tng->hg", kept_hiddens, gate_grads, preferred_element_type=jnp.float32
    )
    return (gate_grads, recur_grad, first_hidden_grad, first_cell_grad)


def neighbour(state, from_upper):
    below = shifted(state, "rows", 1)
    above = shifted(state, "rows", -1)
    return jnp.where(from_upper, above, below)


def chain_forward(gate_all, keeper, out_scale, recur_mat, chain_step, reverse):
    frames, sequences, band_count, gate_width = gate_all.shape
    hidden_width = recur_mat.shape[0]
    starting = chain_step == 0
    row_count = sequences * band_count
    flat_gates = gate_all.reshape(frames, row_count, gate_width)
    flat_keep = jnp.repeat(keeper, band_count, axis=1)
    flat_scale = jnp.repeat(out_scale, band_count)[:, None]
    incoming = jnp.zeros((2, row_count, hidden_width), jnp.float32)
    for step_round in range(CHAIN):
        incoming = jnp.where(starting, 0.0, incoming)
        first_hidden = incoming[0].astype(jnp.bfloat16)
        first_cell = incoming[1]
        hiddens, cells, last_hidden, last_cell = run_block(
            flat_gates, flat_keep, first_hidden, first_cell, recur_mat
        )
        if step_round + 1 < CHAIN:
            outgoing = jnp.stack(
                [last_hidden.astype(jnp.float32) * flat_scale, last_cell * flat_scale]
            )
            incoming = neighbour(outgoing, reverse)
    return (
        hiddens.reshape(frames, sequences, band_count, hidden_width),
        cells.reshape(frames, sequences, band_count, hidden_width),
        first_hidden.reshape(sequences, band_count, hidden_width),
        first_cell.reshape(sequences, band_count, hidden_width),
    )


def chain_backward(
    gate_all,
    keeper,
    out_scale,
    recur_mat,
    hiddens,
    cells,
    first_hidden,
    first_cell,
    hidden_grads,
    chain_step,
    reverse,
):
    frames, sequences, band_count, gate_width = gate_all.shape
    hidden_width = recur_mat.shape[0]
    ending = chain_step == CHAIN - 1
    from_upper = jnp.logical_not(reverse)
    row_count = sequences * band_count
    flat_gates = gate_all.reshape(frames, row_count, gate_width)
    flat_keep = jnp.repeat(keeper, band_count, axis=1)
    flat_scale = jnp.repeat(out_scale, band_count)[:, None]
    flat_hiddens = hiddens.reshape(frames, row_count, hidden_width)
    flat_cells = cells.reshape(frames, row_count, hidden_width)
    flat_grads = hidden_grads.reshape(frames, row_count, hidden_width)
    first_flat_hidden = first_hidden.reshape(row_count, hidden_width)
    first_flat_cell = first_cell.reshape(row_count, hidden_width)
    incoming = jnp.zeros((2, row_count, hidden_width), jnp.float32)
    for step_round in range(CHAIN):
        incoming = jnp.where(ending, 0.0, incoming)
        results = back_block(
            flat_gates,
            flat_keep,
            first_flat_hidden,
            first_flat_cell,
            flat_hiddens,
            flat_cells,
            flat_grads,
            incoming[0] * flat_scale,
            incoming[1] * flat_scale,
            recur_mat,
        )
        if step_round + 1 < CHAIN:
            incoming = neighbour(jnp.stack([results[2], results[3]]), from_upper)
    return (results[0].reshape(frames, sequences, band_count, gate_width), results[1])


def direction_rows(values):
    return lax.all_gather(values, "dir", axis=1, tiled=True)


def direction_back(values):
    return lax.psum_scatter(
        values.astype(jnp.bfloat16), "dir", scatter_dimension=1, tiled=True
    ).astype(jnp.float32)


def project(hidden, weight_pair, bias_row):
    joined = lax.all_to_all(hidden, "dir", split_axis=1, concat_axis=3, tiled=True)
    projected = jnp.einsum("fmbh,hd->fmbd", joined, weight_pair, preferred_element_type=jnp.float32)
    return (projected + bias_row, joined)


def project_back(out_low, joined, weight_pair):
    weight_grad = jnp.einsum("fmbh,fmbd->hd", joined, out_low, preferred_element_type=jnp.float32)
    joined_grad = jnp.einsum(
        "fmbd,hd->fmbh", out_low, weight_pair, preferred_element_type=jnp.float32
    ).astype(jnp.bfloat16)
    hidden_grad = lax.all_to_all(joined_grad, "dir", split_axis=3, concat_axis=1, tiled=True)
    return (hidden_grad.astype(jnp.float32), weight_grad)


def unpack(gain_weight, bias_weight):
    lstm_rows = 16 * H // D
    proj_start = BANDS + lstm_rows
    up_start = proj_start + 2
    down_start = up_start + 4 * BANDS
    return (
        gain_weight[:BANDS],
        gain_weight[BANDS],
        gain_weight[BANDS + 1],
        gain_weight[BANDS + 2 :],
        bias_weight[:BANDS],
        bias_weight[BANDS:proj_start].reshape(4, 4 * H),
        bias_weight[proj_start:up_start],
        bias_weight[up_start:down_start].reshape(BANDS, 4 * D),
        bias_weight[down_start:].reshape(BANDS, 2 * SUBF),
    )


def update(gradient, velocity, weight_now, average, clip_scale, rate):
    clipped = gradient * clip_scale
    velocity_new = MOMENTUM * velocity + clipped
    weight_new = weight_now - rate * (clipped + MOMENTUM * velocity_new)
    average_new = AVERAGE * average + (1.0 - AVERAGE) * weight_new
    return (clipped, velocity_new, weight_new, average_new)


def on_device(
    spectra,
    mask_grad,
    clip_starts,
    split_weight,
    split_velocity,
    split_average,
    lstm_weight,
    lstm_velocity,
    lstm_average,
    proj_weight,
    proj_velocity,
    proj_average,
    up_weight,
    up_velocity,
    up_average,
    down_weight,
    down_velocity,
    down_average,
    gain_weight,
    gain_velocity,
    gain_average,
    bias_weight,
    bias_velocity,
    bias_average,
):
    direction = lax.axis_index("dir")
    reverse = direction == 1
    position = lax.axis_index("rows") % CHAIN
    chain_step = jnp.where(reverse, CHAIN - 1 - position, position)
    gathered = (
        lax.all_gather(split_weight.astype(jnp.bfloat16), "rows", axis=0, tiled=True),
        lax.all_gather(lstm_weight.astype(jnp.bfloat16), "rows", axis=0, tiled=True),
        lax.all_gather(proj_weight.astype(jnp.bfloat16), "rows", axis=0, tiled=True),
        lax.all_gather(up_weight.astype(jnp.bfloat16), "rows", axis=0, tiled=True),
        lax.all_gather(down_weight.astype(jnp.bfloat16), "rows", axis=0, tiled=True),
    )
    split_mat = gathered[0].reshape(BANDS, SUBF, D)
    lstm_mat = gathered[1].reshape(4, D + H, 4 * H)
    proj_mat = gathered[2].reshape(2, 2 * H, D)
    up_mat = gathered[3].reshape(BANDS, D, 4 * D)
    down_mat = gathered[4].reshape(BANDS, 4 * D, 2 * SUBF)
    (
        split_gain,
        time_gain,
        band_gain,
        mask_gain,
        split_bias,
        lstm_bias,
        proj_bias,
        up_bias,
        down_bias,
    ) = unpack(gain_weight, bias_weight)
    time_in = lax.dynamic_index_in_dim(lstm_mat, direction, 0, keepdims=False)
    band_in = lax.dynamic_index_in_dim(lstm_mat, 2 + direction, 0, keepdims=False)
    time_bias = lax.dynamic_index_in_dim(lstm_bias, direction, 0, keepdims=False)
    band_bias = lax.dynamic_index_in_dim(lstm_bias, 2 + direction, 0, keepdims=False)
    spectrum = spectra[0].astype(jnp.float32)
    start_flags = clip_starts[0].astype(jnp.float32)
    frames, sequences = start_flags.shape
    next_flags = jnp.concatenate([start_flags[1:], jnp.zeros((1, sequences), jnp.float32)], axis=0)
    keeper = jnp.where(reverse, (1.0 - next_flags)[::-1], 1.0 - start_flags)
    out_scale = jnp.where(reverse, 1.0 - start_flags[0], jnp.ones((sequences,), jnp.float32))
    normed_low = layer_norm(spectrum, split_gain).astype(jnp.bfloat16)
    embedded = (
        jnp.einsum("fmbs,bsd->fmbd", normed_low, split_mat, preferred_element_type=jnp.float32)
        + split_bias
    )
    time_rows = direction_rows(layer_norm(embedded, time_gain).astype(jnp.bfloat16))
    time_gates = (
        jnp.einsum("fmbd,dg->fmbg", time_rows, time_in[:D], preferred_element_type=jnp.float32)
        + time_bias
    )
    local_gates = jnp.where(reverse, time_gates[::-1], time_gates)
    time_local, time_cells, first_hidden, first_cell = chain_forward(
        local_gates, keeper, out_scale, time_in[D:], chain_step, reverse
    )
    time_hidden = jnp.where(reverse, time_local[::-1], time_local)
    time_out, time_joined = project(time_hidden, proj_mat[0], proj_bias[0])
    after_time = embedded + time_out
    band_rows = direction_rows(layer_norm(after_time, band_gain).astype(jnp.bfloat16))
    band_gates = (
        jnp.einsum("fmbd,dg->bfmg", band_rows, band_in[:D], preferred_element_type=jnp.float32)
        + band_bias
    ).reshape(BANDS, frames * sequences, 4 * H)
    band_local = jnp.where(reverse, band_gates[::-1], band_gates)
    band_keep = jnp.ones((BANDS, frames * sequences), jnp.float32)
    zero_hidden = jnp.zeros((frames * sequences, H), jnp.bfloat16)
    zero_cell = jnp.zeros((frames * sequences, H), jnp.float32)
    band_results = run_block(band_local, band_keep, zero_hidden, zero_cell, band_in[D:])
    band_hidden_local = band_results[0]
    band_cells = band_results[1]
    band_ordered = jnp.where(reverse, band_hidden_local[::-1], band_hidden_local)
    band_hidden = jnp.moveaxis(band_ordered.reshape(BANDS, frames, sequences, H), 0, 2)
    band_out, band_joined = project(band_hidden, proj_mat[1], proj_bias[1])
    after_band = after_time + band_out
    mask_low = layer_norm(after_band, mask_gain).astype(jnp.bfloat16)
    hidden_act = jnp.tanh(
        jnp.einsum("fmbd,bde->fmbe", mask_low, up_mat, preferred_element_type=jnp.float32) + up_bias
    )
    act_low = hidden_act.astype(jnp.bfloat16)
    output_pre = (
        jnp.einsum("fmbe,bes->fmbs", act_low, down_mat, preferred_element_type=jnp.float32)
        + down_bias
    )
    value_part = output_pre[..., :SUBF]
    gate_part = jax.nn.sigmoid(output_pre[..., SUBF:])
    band_mask = value_part * gate_part
    cotangent = mask_grad[0].astype(jnp.float32)
    output_grad = jnp.concatenate(
        [cotangent * gate_part, cotangent * value_part * gate_part * (1.0 - gate_part)], axis=-1
    ).astype(jnp.bfloat16)
    down_bias_grad = jnp.sum(output_grad, axis=(0, 1), dtype=jnp.float32)
    down_grad = jnp.einsum(
        "fmbe,fmbs->bes", act_low, output_grad, preferred_element_type=jnp.float32
    )
    act_grad = jnp.einsum(
        "fmbs,bes->fmbe", output_grad, down_mat, preferred_element_type=jnp.float32
    )
    pre_grad = (act_grad * (1.0 - hidden_act * hidden_act)).astype(jnp.bfloat16)
    up_bias_grad = jnp.sum(pre_grad, axis=(0, 1), dtype=jnp.float32)
    up_grad = jnp.einsum("fmbd,fmbe->bde", mask_low, pre_grad, preferred_element_type=jnp.float32)
    mask_in_grad = jnp.einsum(
        "fmbe,bde->fmbd", pre_grad, up_mat, preferred_element_type=jnp.float32
    )
    after_band_grad, mask_gain_grad = norm_back(after_band, mask_gain, mask_in_grad, (0, 1))
    band_out_low = after_band_grad.astype(jnp.bfloat16)
    band_proj_bias_grad = jnp.sum(band_out_low, axis=(0, 1, 2), dtype=jnp.float32)
    band_hidden_grad, band_proj_grad = project_back(band_out_low, band_joined, proj_mat[1])
    band_grad_rows = jnp.moveaxis(band_hidden_grad, 2, 0).reshape(BANDS, frames * sequences, H)
    band_grad_local = jnp.where(reverse, band_grad_rows[::-1], band_grad_rows)
    band_back = back_block(
        band_local,
        band_keep,
        zero_hidden,
        zero_cell,
        band_hidden_local,
        band_cells,
        band_grad_local,
        zero_cell,
        zero_cell,
        band_in[D:],
    )
    band_gate_grad = jnp.where(reverse, band_back[0][::-1], band_back[0]).reshape(
        BANDS, frames, sequences, 4 * H
    )
    band_recur_grad = band_back[1]
    band_lstm_bias_grad = jnp.sum(band_gate_grad, axis=(0, 1, 2), dtype=jnp.float32)
    band_input_grad = jnp.einsum(
        "fmbd,bfmg->dg", band_rows, band_gate_grad, preferred_element_type=jnp.float32
    )
    band_rows_grad = jnp.einsum(
        "bfmg,dg->fmbd", band_gate_grad, band_in[:D], preferred_element_type=jnp.float32
    )
    banded_grad = direction_back(band_rows_grad)
    after_time_norm_grad, band_gain_grad = norm_back(after_time, band_gain, banded_grad, (0, 1, 2))
    after_time_grad = after_band_grad + after_time_norm_grad
    time_out_low = after_time_grad.astype(jnp.bfloat16)
    time_proj_bias_grad = jnp.sum(time_out_low, axis=(0, 1, 2), dtype=jnp.float32)
    time_hidden_grad, time_proj_grad = project_back(time_out_low, time_joined, proj_mat[0])
    local_hidden_grad = jnp.where(reverse, time_hidden_grad[::-1], time_hidden_grad)
    time_gate_local, time_recur_grad = chain_backward(
        local_gates,
        keeper,
        out_scale,
        time_in[D:],
        time_local,
        time_cells,
        first_hidden,
        first_cell,
        local_hidden_grad,
        chain_step,
        reverse,
    )
    time_gate_grad = jnp.where(reverse, time_gate_local[::-1], time_gate_local)
    time_lstm_bias_grad = jnp.sum(time_gate_grad, axis=(0, 1, 2), dtype=jnp.float32)
    time_input_grad = jnp.einsum(
        "fmbd,fmbg->dg", time_rows, time_gate_grad, preferred_element_type=jnp.float32
    )
    time_rows_grad = jnp.einsum(
        "fmbg,dg->fmbd", time_gate_grad, time_in[:D], preferred_element_type=jnp.float32
    )
    timed_grad = direction_back(time_rows_grad)
    embedded_norm_grad, time_gain_grad = norm_back(embedded, time_gain, timed_grad, (0, 1, 2))
    embedded_low = (after_time_grad + embedded_norm_grad).astype(jnp.bfloat16)
    split_bias_grad = jnp.sum(embedded_low, axis=(0, 1), dtype=jnp.float32)
    split_grad = jnp.einsum(
        "fmbs,fmbd->bsd", normed_low, embedded_low, preferred_element_type=jnp.float32
    )
    normed_grad = jnp.einsum(
        "fmbd,bsd->fmbs", embedded_low, split_mat, preferred_element_type=jnp.float32
    )
    spectra_grad, split_gain_grad = norm_back(spectrum, split_gain, normed_grad, (0, 1))
    lstm_grads = jnp.zeros((4, D + H, 4 * H), jnp.float32)
    lstm_grads = lax.dynamic_update_index_in_dim(
        lstm_grads, jnp.concatenate([time_input_grad, time_recur_grad], axis=0), direction, 0
    )
    lstm_grads = lax.dynamic_update_index_in_dim(
        lstm_grads, jnp.concatenate([band_input_grad, band_recur_grad], axis=0), 2 + direction, 0
    )
    lstm_bias_grad = jnp.zeros((4, 4 * H), jnp.float32)
    lstm_bias_grad = lax.dynamic_update_index_in_dim(
        lstm_bias_grad, time_lstm_bias_grad, direction, 0
    )
    lstm_bias_grad = lax.dynamic_update_index_in_dim(
        lstm_bias_grad, band_lstm_bias_grad, 2 + direction, 0
    )
    gain_local = jnp.concatenate(
        [split_gain_grad, time_gain_grad[None], band_gain_grad[None], mask_gain_grad], axis=0
    )
    bias_local = jnp.concatenate(
        [
            split_bias_grad,
            lstm_bias_grad.reshape(16 * H // D, D),
            jnp.stack([time_proj_bias_grad, band_proj_bias_grad]),
            up_bias_grad.reshape(4 * BANDS, D),
            down_bias_grad.reshape(2 * BANDS, D),
        ],
        axis=0,
    )
    split_local = split_grad.reshape(BANDS * SUBF, D)
    lstm_local = lstm_grads.reshape(4 * (D + H), 4 * H)
    proj_local = jnp.stack([time_proj_grad, band_proj_grad]).reshape(4 * H, D)
    up_local = up_grad.reshape(BANDS * D, 4 * D)
    down_local = down_grad.reshape(4 * BANDS * D, 2 * SUBF)
    gain_total, bias_total = lax.psum((gain_local, bias_local), ("dir", "rows"))
    row_shards = (
        lax.psum_scatter(split_local, "rows", scatter_dimension=0, tiled=True),
        lax.psum_scatter(lstm_local, "rows", scatter_dimension=0, tiled=True),
        lax.psum_scatter(proj_local, "rows", scatter_dimension=0, tiled=True),
        lax.psum_scatter(up_local, "rows", scatter_dimension=0, tiled=True),
        lax.psum_scatter(down_local, "rows", scatter_dimension=0, tiled=True),
    )
    shards = (
        lax.psum(row_shards[0].astype(jnp.bfloat16), "dir").astype(jnp.float32),
        lax.psum(row_shards[1].astype(jnp.bfloat16), "dir").astype(jnp.float32),
        lax.psum(row_shards[2].astype(jnp.bfloat16), "dir").astype(jnp.float32),
        lax.psum(row_shards[3].astype(jnp.bfloat16), "dir").astype(jnp.float32),
        lax.psum(row_shards[4].astype(jnp.bfloat16), "dir").astype(jnp.float32),
    )
    shard_square = sum((jnp.sum(shard_part * shard_part) for shard_part in shards))
    big_square = lax.psum(shard_square, "rows")
    total_square = big_square + jnp.sum(gain_total * gain_total) + jnp.sum(bias_total * bias_total)
    grad_norm = jnp.sqrt(total_square)
    clip_scale = jnp.minimum(1.0, CLIP_NORM / (grad_norm + 1e-06))
    outputs = (band_mask.astype(jnp.bfloat16)[None], spectra_grad[None], grad_norm)
    outputs = outputs + update(
        shards[0], split_velocity, split_weight, split_average, clip_scale, LEARN_RATE
    )
    outputs = outputs + update(
        shards[1], lstm_velocity, lstm_weight, lstm_average, clip_scale, LEARN_RATE
    )
    outputs = outputs + update(
        shards[2], proj_velocity, proj_weight, proj_average, clip_scale, LEARN_RATE
    )
    outputs = outputs + update(
        shards[3], up_velocity, up_weight, up_average, clip_scale, LEARN_RATE
    )
    outputs = outputs + update(
        shards[4], down_velocity, down_weight, down_average, clip_scale, LEARN_RATE
    )
    outputs = outputs + update(
        gain_total, gain_velocity, gain_weight, gain_average, clip_scale, GAIN_RATE
    )
    outputs = outputs + update(
        bias_total, bias_velocity, bias_weight, bias_average, clip_scale, GAIN_RATE
    )
    return outputs


def solution(mesh):
    return jax.shard_map(
        on_device,
        mesh=mesh,
        in_specs=(
            P("rows", None, "dir", None, None),
            P("rows", None, "dir", None, None),
            P("rows", None, None),
            P("rows", None),
            P("rows", None),
            P("rows", None),
            P("rows", None),
            P("rows", None),
            P("rows", None),
            P("rows", None),
            P("rows", None),
            P("rows", None),
            P("rows", None),
            P("rows", None),
            P("rows", None),
            P("rows", None),
            P("rows", None),
            P("rows", None),
            P(),
            P(),
            P(),
            P(),
            P(),
            P(),
        ),
        out_specs=(
            P("rows", None, "dir", None, None),
            P("rows", None, "dir", None, None),
            P(),
            P("rows", None),
            P("rows", None),
            P("rows", None),
            P("rows", None),
            P("rows", None),
            P("rows", None),
            P("rows", None),
            P("rows", None),
            P("rows", None),
            P("rows", None),
            P("rows", None),
            P("rows", None),
            P("rows", None),
            P("rows", None),
            P("rows", None),
            P("rows", None),
            P("rows", None),
            P("rows", None),
            P("rows", None),
            P("rows", None),
            P(),
            P(),
            P(),
            P(),
            P(),
            P(),
            P(),
            P(),
        ),
        check_vma=False,
    )
```

profile of v0, /device:TPU:0, one launch (start us, length us, event | category | flops | bytes accessed | tf_op | source)
XLA Modules:
  0.0 4136.3 jit_solution(3590276301963867860)
XLA Ops:
  14.7 56.6 %all-gather.7.cloned.1.call-done = bf16[5248,128]{1,0:T(8,128)(2,1)} async-done(((bf16[328,128]{1,0:T(8,128)(2,1)}), bf16[5248,128]{1,0:T(8,128)(2,1)}) %all-gather.7.cloned.1.call-update) | async-done | bytes 1343504 | tf_op jit(solution)/shard_map/all_gather | solution.py:292
  85.0 72.7 %all-gather.11.cloned.1.call-done = bf16[1536,1024]{1,0:T(8,128)(2,1)} async-done(((bf16[96,1024]{1,0:T(8,128)(2,1)}), bf16[1536,1024]{1,0:T(8,128)(2,1)}) %all-gather.11.cloned.1.call-update) | async-done | bytes 3145744 | tf_op jit(solution)/shard_map/all_gather | solution.py:293
  169.1 31.9 rev.27
  238.6 89.9 %while.168 = (s32[]{:T(128)}, bf16[82,256]{1,0:T(8,128)(2,1)S(1)}, f32[82,256]{1,0:T(8,128)S(1)}, f32[64,82,1024]{2,1,0:T(8,128)}, f32[64,82]{1,0:T(8,128)S(1)},...) while((s32[]{:T(128)}, bf16[82,256]{1,0:T(8,128)(2,1)S(1)}, f32[82,256]{1,0:T(8,128)S(1)}, ...), condition=%wide.region_5.6_spmd.clone, body=%wide.region_4.5_spmd.clone.sunk | while | flops 43453524 | bytes 1785232 | solution.py:68
  339.5 90.1 %while.161 = (s32[]{:T(128)}, bf16[82,256]{1,0:T(8,128)(2,1)S(1)}, f32[82,256]{1,0:T(8,128)S(1)}, f32[64,82,1024]{2,1,0:T(8,128)}, f32[64,82]{1,0:T(8,128)S(1)}, /*index=5*/bf16[256,1024]{1,0:T(8,128)(2,1)S(1)}, s32[]{:T(128)}) while((s32[]{:T(128)}, bf16[82,256]{1,0:T(8,128)(2,1)S(1)}, f32[82,256]{1,0:T(8,128)S(1)}, ...), condition=%wide.region_7.8_spmd, body=%wide.region_6.7_spmd.sunk | while | flops 43411540 | bytes 1785213 | solution.py:68
  441.7 90.1 %while.162 = (s32[]{:T(128)}, bf16[82,256]{1,0:T(8,128)(2,1)S(1)}, f32[82,256]{1,0:T(8,128)S(1)}, f32[64,82,1024]{2,1,0:T(8,128)}, f32[64,82]{1,0:T(8,128)S(1)}, /*index=5*/bf16[256,1024]{1,0:T(8,128)(2,1)S(1)}, s32[]{:T(128)}) while((s32[]{:T(128)}, bf16[82,256]{1,0:T(8,128)(2,1)S(1)}, f32[82,256]{1,0:T(8,128)S(1)}, ...), condition=%wide.region_9.10_spmd, body=%wide.region_8.9_spmd.sunk | while | flops 43411540 | bytes 1785213 | solution.py:68
  539.7 39.8 all_gather.24
  582.9 169.0 %while.163 = (s32[]{:T(128)}, bf16[82,256]{1,0:T(8,128)(2,1)S(1)}, f32[82,256]{1,0:T(8,128)S(1)}, bf16[64,82,256]{2,1,0:T(8,128)(2,1)}, f32[64,82,256]{2,1,0:T(8...) while((s32[]{:T(128)}, bf16[82,256]{1,0:T(8,128)(2,1)S(1)}, ...), condition=%wide.region_11.12_spmd, body=%wide.region_10.11_spmd.sunk | while | flops 43411540 | bytes 2004373 | solution.py:68
  805.9 36.8 copy.194
  842.7 26.2 reshape.806
  892.6 112.9 %while.169 = (s32[]{:T(128)}, bf16[128,256]{1,0:T(8,128)(2,1)S(1)}, f32[128,256]{1,0:T(8,128)S(1)}, bf16[41,128,256]{2,1,0:T(8,128)(2,1)}, f32[41,128,256]{2,1,0...) while((s32[]{:T(128)}, bf16[128,256]{1,0:T(8,128)(2,1)S(1)}, ...), condition=%wide.region_15.16_spmd.clone, body=%wide.region_14.15_spmd.clone.sunk | while | flops 67764224 | bytes 2818172 | solution.py:68
  1165.5 245.0 %while.170 = (s32[]{:T(128)}, f32[128,256]{1,0:T(8,128)S(1)}, f32[128,256]{1,0:T(8,128)S(1)}, bf16[41,128,1024]{2,1,0:T(8,128)(2,1)}, bf16[41,128,256]{2,1,0:T(8...) while((s32[]{:T(128)}, f32[128,256]{1,0:T(8,128)S(1)}, ...), condition=%wide.region_21.22_spmd.clone, body=%wide.region_20.21_spmd.clone.sunk | while | flops 137756672 | bytes 5178547 | solution.py:117
  1542.5 276.0 %while.164 = (s32[]{:T(128)}, f32[82,256]{1,0:T(8,128)S(1)}, f32[82,256]{1,0:T(8,128)S(1)}, f32[64,82,256]{2,1,0:T(8,128)}, f32[64,82,1024]{2,1,0:T(8,128)}, /*i...) while((s32[]{:T(128)}, f32[82,256]{1,0:T(8,128)S(1)}, ...), condition=%wide.region_26.27_spmd, body=%wide.region_25.26_spmd.sunk | while | flops 87641680 | bytes 3304517 | solution.py:117
  1832.9 276.1 %while.165 = (s32[]{:T(128)}, f32[82,256]{1,0:T(8,128)S(1)}, f32[82,256]{1,0:T(8,128)S(1)}, f32[64,82,256]{2,1,0:T(8,128)}, f32[64,82,1024]{2,1,0:T(8,128)}, /*i...) while((s32[]{:T(128)}, f32[82,256]{1,0:T(8,128)S(1)}, ...), condition=%wide.region_28.29_spmd, body=%wide.region_27.28_spmd.sunk | while | flops 87641680 | bytes 3304517 | solution.py:117
  2121.4 276.1 %while.166 = (s32[]{:T(128)}, f32[82,256]{1,0:T(8,128)S(1)}, f32[82,256]{1,0:T(8,128)S(1)}, f32[64,82,256]{2,1,0:T(8,128)}, f32[64,82,1024]{2,1,0:T(8,128)}, /*i...) while((s32[]{:T(128)}, f32[82,256]{1,0:T(8,128)S(1)}, ...), condition=%wide.region_30.31_spmd, body=%wide.region_29.30_spmd.sunk | while | flops 87641680 | bytes 3304517 | solution.py:117
  2418.5 414.4 %while.167 = (s32[]{:T(128)}, f32[82,256]{1,0:T(8,128)S(1)}, f32[82,256]{1,0:T(8,128)S(1)}, bf16[64,82,1024]{2,1,0:T(8,128)(2,1)}, bf16[64,82,256]{2,1,0:T(8,128...) while((s32[]{:T(128)}, f32[82,256]{1,0:T(8,128)S(1)}, ...), condition=%wide.region_32.33_spmd, body=%wide.region_31.32_spmd.sunk | while | flops 88397392 | bytes 3742977 | solution.py:117
  2845.6 28.9 rev.35
  2986.7 76.7 %reduce-scatter.23.cloned.1.call-done = f32[328,128]{1,0:T(8,128)} async-done(((f32[5248,128]{1,0:T(8,128)}), f32[328,128]{1,0:T(8,128)}) %reduce-scatter.23.cloned.1.call-update) | async-done | bytes 167952
  3064.9 146.7 %reduce-scatter.15.cloned.1.call-done = f32[96,1024]{1,0:T(8,128)} async-done(((f32[1536,1024]{1,0:T(8,128)}), f32[96,1024]{1,0:T(8,128)}) %reduce-scatter.15.cloned.1.call-update) | async-done | bytes 393232 | tf_op jit(solution)/shard_map/reduce_scatter | solution.py:489
  3213.3 224.7 %reduce-scatter.19.cloned.1.call-done = f32[328,512]{1,0:T(8,128)} async-done(((f32[5248,512]{1,0:T(8,128)}), f32[328,512]{1,0:T(8,128)}) %reduce-scatter.19.cloned.1.call-update) | async-done | bytes 671760 | tf_op jit(solution)/shard_map/reduce_scatter | solution.py:491
  3439.9 445.6 %reduce-scatter.21.cloned.1.call-done = f32[1312,256]{1,0:T(8,128)} async-done(((f32[20992,256]{1,0:T(8,128)}), f32[1312,256]{1,0:T(8,128)}) %reduce-scatter.21.cloned.1.call-update) | async-done | bytes 1343504 | tf_op jit(solution)/shard_map/reduce_scatter | solution.py:492
  3900.0 45.8 %psum.62 = f32[84,128]{1,0:T(8,128)S(1)} all-reduce(f32[84,128]{1,0:T(8,128)S(1)} %pad_maximum_fusion.12), channel_id=1, replica_groups=mesh['dir'=2,'rows'=16] {'dir','rows'}, use_global_device_ids=true, to_apply=%region_58.59 | all-reduce | flops 10752 | bytes 86016 | tf_op jit(solution)/shard_map/psum | solution.py:486
  3956.9 112.8 %all-reduce.8.cloned.1.call-done = f32[321,128]{1,0:T(8,128)} async-done(((f32[321,128]{1,0:T(8,128)}), f32[321,128]{1,0:T(8,128)}) %all-reduce.8.cloned.1.call-update) | async-done | bytes 164368 | tf_op jit(solution)/shard_map/psum | solution.py:486
  4071.2 43.3 %psum.61 = f32[]{:T(128)} all-reduce(f32[]{:T(128)S(6)} %add.789), channel_id=1, replica_groups=mesh['dir'=2,'rows'=16] {'rows'}, use_global_device_ids=true, to_apply=%region_53.54 | all-reduce | flops 1 | bytes 8 | tf_op jit(solution)/shard_map/psum | solution.py:502
  (3084 shorter events, 2710.3 us)
Async XLA Ops:
  7.2 64.1 %all-gather.7.cloned.1.call-start = ((), (), s32[]{:S(2)}) async-start(), calls=%async_computation.11 | async-start | bytes 1427456 | tf_op jit(solution)/shard_map/all_gather | solution.py:292
  8.8 76.1 %all-gather.9.cloned.1.call-start = ((), (), s32[]{:S(2)}) async-start(), calls=%async_computation.12 | async-start | bytes 2015232 | tf_op jit(solution)/shard_map/all_gather | solution.py:211
  76.5 81.2 %all-gather.11.cloned.1.call-start = ((), (), s32[]{:S(2)}) async-start(), calls=%async_computation.13 | async-start | bytes 3342336 | tf_op jit(solution)/shard_map/all_gather | solution.py:293
  77.3 717.1 %all-gather.13.cloned.1.call-start = ((), (), s32[]{:S(2)}) async-start(), calls=%async_computation.14 | async-start | bytes 2015232 | tf_op jit(solution)/shard_map/all_gather | solution.py:211
  329.9 9.5 collective-permute-start.1
  431.0 10.6 collective-permute-start.3
  531.9 47.6 %collective-permute-start.4 = (f32[2,82,256]{2,1,0:T(8,128)S(1)}, f32[2,82,256]{2,1,0:T(8,128)S(1)}, u32[]{:S(2)}, u32[]{:S(2)}) collective-permute-start(f32[2,82,256]{2,1,0:T(8,128)S(1)} %pad_maximum_fusion.8), channel_id=1, source_target_pairs={{1,0},{2,1},{3,2},{4,3},{5,4},{6,5},{7,6},{8,7},{9,8},{10,9},{11,1... | collective-permute-start | bytes 503816 | tf_op jit(solution)/shard_map/ppermute | solution.py:24
  533.2 46.3 %collective-permute-start.5 = (f32[2,82,256]{2,1,0:T(8,128)S(1)}, f32[2,82,256]{2,1,0:T(8,128)}, u32[]{:S(2)}, u32[]{:S(2)}) collective-permute-start(f32[2,82,256]{2,1,0:T(8,128)S(1)} %pad_maximum_fusion.8), channel_id=1, source_target_pairs={{0,1},{1,2},{2,3},{3,4},{4,5},{5,6},{6,7},{7,8},{8,9},{9,10},{10,1... | collective-permute-start | bytes 503816 | tf_op jit(solution)/shard_map/ppermute | solution.py:24
  788.8 259.9 %all-gather.15.cloned.1.call-start = ((), (), s32[]{:S(2)}) async-start(), calls=%async_computation.15 | async-start | bytes 5709824 | tf_op jit(solution)/shard_map/all_gather | solution.py:295
  789.7 265.0 %all-gather.17.cloned.1.call-start = ((), (), s32[]{:S(2)}) async-start(), calls=%async_computation.16 | async-start | bytes 11419648 | tf_op jit(solution)/shard_map/all_gather | solution.py:296
  790.7 675.5 %reduce-scatter.11.cloned.1.call-start = ((), (), s32[]{:S(2)}) async-start(), calls=%async_computation.17 | async-start | bytes 2015232 | tf_op jit(solution)/shard_map/reduce_scatter | solution.py:215
  1455.5 1445.7 %reduce-scatter.13.cloned.1.call-start = ((), (), s32[]{:S(2)}) async-start(), calls=%async_computation.18 | async-start | bytes 2015232 | tf_op jit(solution)/shard_map/reduce_scatter | solution.py:215
  1819.9 13.0 collective-permute-start.7
  2109.1 9.2 collective-permute-start.8
  2110.4 10.9 collective-permute-start.9
  2397.5 9.1 collective-permute-start.10
  2398.8 12.1 collective-permute-start.11
  2892.0 90.0 %reduce-scatter.17.cloned.1.call-start = ((), (), s32[]{:S(2)}) async-start(), calls=%async_computation.20 | async-start | bytes 557056 | tf_op jit(solution)/shard_map/reduce_scatter | solution.py:490
  2896.8 166.5 %reduce-scatter.23.cloned.1.call-start = ((), (), s32[]{:S(2)}) async-start(), calls=%async_computation.24 | async-start | bytes 2854912
  2913.2 298.4 %reduce-scatter.15.cloned.1.call-start = ((), (), s32[]{:S(2)}) async-start(), calls=%async_computation.19 | async-start | bytes 6684672 | tf_op jit(solution)/shard_map/reduce_scatter | solution.py:489
  2938.3 499.8 %reduce-scatter.19.cloned.1.call-start = ((), (), s32[]{:S(2)}) async-start(), calls=%async_computation.21 | async-start | bytes 11419648 | tf_op jit(solution)/shard_map/reduce_scatter | solution.py:491
  2946.5 939.0 %reduce-scatter.21.cloned.1.call-start = ((), (), s32[]{:S(2)}) async-start(), calls=%async_computation.22 | async-start | bytes 22839296 | tf_op jit(solution)/shard_map/reduce_scatter | solution.py:492
  2960.6 985.9 %all-reduce.10.cloned.1.call-start = ((), (), s32[]{:S(2)}) async-start(), calls=%async_computation.25 | async-start | bytes 2576384 | tf_op jit(solution)/shard_map/psum | solution.py:495
  3887.8 181.9 %all-reduce.8.cloned.1.call-start = ((), (), s32[]{:S(2)}) async-start(), calls=%async_computation.23 | async-start | bytes 335872 | tf_op jit(solution)/shard_map/psum | solution.py:486
  (108 other events, 8355.2 us)
Sparse Core Ops, SparseCore 0:
  11.4 59.8 all-gather.6
  76.6 8.3 all-gather.8
  88.3 69.2 all-gather.10
  789.0 5.3 all-gather.12
  797.5 87.2 all-gather.14
  887.9 133.2 all-gather.16
  1455.6 10.0 reduce-scatter.10
  2892.1 9.0 reduce-scatter.12
  2904.1 77.8 reduce-scatter.16
  2984.2 79.1 reduce-scatter.22
  3068.6 142.9 reduce-scatter.14
  3213.8 224.1 reduce-scatter.18
  3440.5 445.0 reduce-scatter.20
  3890.5 26.5 all-reduce.9
  3946.6 123.0 all-reduce.7
where the time goes:
time: 4200 us; the launch traced here: 4140 us
  other arithmetic  1280 us (30%)
  waiting for transfers between devices  1200 us (29%)
  matrix products  967 us (23%)
  local copies, waits for them, and re-layouts  449 us (11%)
  blocking collectives  163 us (4%)
    reduce_scatter x1, waiting for transfers between devices, on_device(): lax.psum_scatter(down_local, 'rows', scatter_dimension=0, tiled=True)  446 us
    dot_general x297, matrix products, retreat(): jnp.dot(kept_hidden, recur_mat, preferred_element_type=jnp.float32)  378 us
    dot_general x297, matrix products, advance(): jnp.dot(kept_hidden, recur_mat, preferred_element_type=jnp.float32)  371 us
    mul x297, other arithmetic, retreat(): prev_cell_grad = cell_total * forget * keep_col  310 us
    another operation x298, other arithmetic  296 us
    dynamic_update_slice x274, other arithmetic, run_block(): lax.scan(advance, (first_hidden, first_cell), (gate_in, keeper))  244 us
    reduce_scatter x1, waiting for transfers between devices, on_device(): lax.psum_scatter(up_local, 'rows', scatter_dimension=0, tiled=True)  225 us
    convert_element_type x256, other arithmetic, retreat(): kept_hidden = hidden_prev * keep_col.astype(jnp.bfloat16)  178 us
  transfers between devices with their start and end apart: 27, of which 21 were waited for; matrix products, arithmetic and copies ran while one was open for 9% of the time, Pallas kernels for 0%

commit v1 on v0

v1 whole, which is shorter than its diff:
```python
import functools

import jax
import jax.numpy as jnp
import numpy as np
from jax import lax
from jax.experimental import pallas as pl
from jax.experimental.pallas import tpu as pltpu
from jax.sharding import PartitionSpec as P

D = 128
H = 256
G4 = 4 * H
BANDS = 41
SUBF = 128
CHAIN = 4
SLOTS = 11
STRIDE = 10
ROWS_T = 16
STEPS_B = 42
VMEM = 60 << 20

EPSILON = 1e-05
MOMENTUM = 0.9
LEARN_RATE = 5.0
GAIN_RATE = 50.0
AVERAGE = 0.5
CLIP_NORM = 5.0

BF = jnp.bfloat16
F32 = jnp.float32


def mm(a, b):
    return jnp.dot(a, b, preferred_element_type=F32)


def mm_nt(a, b):
    return lax.dot_general(a, b, (((1,), (1,)), ((), ())), preferred_element_type=F32)


def mm_tn(a, b):
    return lax.dot_general(a, b, (((0,), (0,)), ((), ())), preferred_element_type=F32)


def ln(v):
    c = v - jnp.mean(v, axis=-1, keepdims=True)
    r = lax.rsqrt(jnp.mean(c * c, axis=-1, keepdims=True) + EPSILON)
    return c * r, r


def ln_back(n, r, gain, dy):
    dg = dy * gain
    return r * (
        dg - jnp.mean(dg, axis=-1, keepdims=True) - n * jnp.mean(dg * n, axis=-1, keepdims=True)
    )


def rowsum(v):
    return jnp.sum(v, axis=0, keepdims=True)


def forward_chunk(keep, x_ref, w_ref, b_ref, outs, gates, hk_s, ck_s, steps, chunk, rows, unroll, hall):
    n = steps // chunk
    j = pl.program_id(0)
    first = (j * chunk, (n - 1 - j) * chunk)

    @pl.when(j == 0)
    def _():
        hk_s[...] = jnp.zeros_like(hk_s)
        ck_s[...] = jnp.zeros_like(ck_s)

    for d in range(2):
        x = x_ref[pl.ds(pl.multiple_of(first[d] * rows, chunk * rows), chunk * rows), :]
        gates[d] = mm(x, w_ref[d, :D]) + b_ref[d]

    def step(t, carry):
        new = []
        for d in range(2):
            hk, ck = carry[2 * d], carry[2 * d + 1]
            tt = t if d == 0 else chunk - 1 - t
            at = first[d] + tt
            now = keep[d * steps + at]
            later = jnp.minimum(at + 1, steps - 1) if d == 0 else jnp.maximum(at - 1, 0)
            nxt = keep[d * steps + later]
            h_ref, hk_ref, cf_ref = outs[3 * d : 3 * d + 3]
            a = gates[d, pl.ds(pl.multiple_of(tt * rows, rows), rows), :] + mm(hk, w_ref[d, D:])
            ti = jnp.tanh(a[:, :H])
            tf = jnp.tanh(a[:, H : 2 * H])
            g = jnp.tanh(a[:, 2 * H : 3 * H])
            to = jnp.tanh(a[:, 3 * H :])
            i = 0.5 * ti + 0.5
            f = 0.5 * tf + 0.5
            o = 0.5 * to + 0.5
            c = f * ck + i * g
            tc = jnp.tanh(c)
            h = o * tc
            h_low = h.astype(BF)
            hk_ref[tt] = hk
            h_ref[tt] = h_low
            if hall is not None:
                hall[d, pl.ds(pl.multiple_of(at * rows, rows), rows), :] = h_low
            cf_ref[tt, :, :H] = o * (1.0 - tc * tc)
            cf_ref[tt, :, H : 2 * H] = g * (0.5 - 0.5 * ti * ti)
            cf_ref[tt, :, 2 * H : 3 * H] = ck * (0.5 - 0.5 * tf * tf)
            cf_ref[tt, :, 3 * H : 4 * H] = i * (1.0 - g * g)
            cf_ref[tt, :, 4 * H : 5 * H] = tc * (0.5 - 0.5 * to * to)
            cf_ref[tt, :, 5 * H :] = f * now
            new += [(h * nxt).astype(BF), c * nxt]
        return tuple(new)

    done = lax.fori_loop(
        0, chunk, step, (hk_s[0], ck_s[0], hk_s[1], ck_s[1]), unroll=unroll
    )
    for d in range(2):
        hk_s[d] = done[2 * d]
        ck_s[d] = done[2 * d + 1]


def backward_chunk(
    keep, x_ref, ol, w_ref, p_ref, ins, dw, dp, db, wt, pt, da, sh, rg, ch_s, cc_s, steps, chunk, rows, unroll
):
    n = steps // chunk
    j = pl.program_id(0)
    first = ((n - 1 - j) * chunk, j * chunk)
    span = chunk * rows

    @pl.when(j == 0)
    def _():
        ch_s[...] = jnp.zeros_like(ch_s)
        cc_s[...] = jnp.zeros_like(cc_s)
        rg[...] = jnp.zeros_like(rg)
        dw[...] = jnp.zeros_like(dw)
        dp[...] = jnp.zeros_like(dp)
        db[...] = jnp.zeros_like(db)
        for d in range(2):
            wt[d] = w_ref[d].T
            pt[d] = p_ref[pl.ds(d * H, H), :].T

    at_rows = [pl.ds(pl.multiple_of(first[d] * rows, span), span) for d in range(2)]
    for d in range(2):
        sh[d] = mm(ol[at_rows[d], :], pt[d]).astype(BF)

    def step(t, carry):
        new = []
        for d in range(2):
            ch, cc = carry[2 * d], carry[2 * d + 1]
            tt = chunk - 1 - t if d == 0 else t
            now = keep[d * steps + first[d] + tt]
            cf = ins[3 * d + 2]
            here = pl.ds(pl.multiple_of(tt * rows, rows), rows)
            dh = sh[d, here, :].astype(F32) + ch
            dc = cc + dh * cf[tt, :, :H]
            da_now = jnp.concatenate(
                [
                    (dc * cf[tt, :, H : 2 * H]).astype(BF),
                    (dc * cf[tt, :, 2 * H : 3 * H]).astype(BF),
                    (dc * cf[tt, :, 3 * H : 4 * H]).astype(BF),
                    (dh * cf[tt, :, 4 * H : 5 * H]).astype(BF),
                ],
                axis=-1,
            )
            da[d, here, :] = da_now
            new += [mm(da_now, wt[d, :, D:]) * now, dc * cf[tt, :, 5 * H :]]
        return tuple(new)

    done = lax.fori_loop(0, chunk, step, (ch_s[0], cc_s[0], ch_s[1], cc_s[1]), unroll=unroll)
    ones = jnp.ones((8, span), BF)
    for d in range(2):
        ch_s[d] = done[2 * d]
        cc_s[d] = done[2 * d + 1]
        here = at_rows[d]
        grad = da[d]
        rg[here, :] = rg[here, :] + mm(grad, wt[d, :, :D])
        dw[d, :D, :] = dw[d, :D, :] + mm_tn(x_ref[here, :], grad)
        dw[d, D:, :] = dw[d, D:, :] + mm_tn(ins[3 * d + 1][...].reshape(span, H), grad)
        db[d] = db[d] + mm(ones, grad)
        at_p = pl.ds(d * H, H)
        dp[at_p, :] = dp[at_p, :] + mm_tn(ins[3 * d][...].reshape(span, H), ol[here, :])


def time_forward_kernel(
    steps, chunk, keep, sp, sm, sg, sb, tg, bg, w, b, p, pb,
    emb, at, br, xs, h0, hk0, cf0, h1, hk1, cf1,
    gates, hk_s, ck_s, xt, hall,
):
    n = steps // chunk
    j = pl.program_id(0)
    frames = sp.shape[2]

    @pl.when(j == 0)
    def _():
        xt[...] = jnp.zeros_like(xt)
        for k in range(SLOTS):
            v = sp[:, k].reshape(steps, D).astype(F32)
            normed = (ln(v)[0] * sg[pl.ds(k, 1), :]).astype(BF)
            e = mm(normed, sm[k]) + sb[pl.ds(k, 1), :]
            emb[:, k] = e.reshape(CHAIN, frames, D)
            xt[pl.ds(k, steps, stride=ROWS_T), :] = ln(e)[0] * tg[...]
        xs[...] = xt[...].astype(BF)

    forward_chunk(
        keep, xs, w, b, (h0, hk0, cf0, h1, hk1, cf1), gates, hk_s, ck_s, steps, chunk, ROWS_T, 4, hall
    )

    @pl.when(j == n - 1)
    def _():
        span = 512
        for s in range(0, steps * ROWS_T, span):
            here = pl.ds(s, span)
            xt[here, :] = mm(hall[0, here, :], p[:H]) + mm(hall[1, here, :], p[H:])
        for k in range(SLOTS):
            to = xt[pl.ds(k, steps, stride=ROWS_T), :] + pb[...]
            a = emb[:, k].reshape(steps, D) + to
            at[:, k] = a.reshape(CHAIN, frames, D)
            br[:, k] = (ln(a)[0] * bg[...]).astype(BF).reshape(CHAIN, frames, D)


def band_forward_kernel(
    steps, chunk, keep, rows_in, w, b, p,
    bo, xs, h0, hk0, cf0, h1, hk1, cf1,
    gates, hk_s, ck_s, hall,
):
    n = steps // chunk
    j = pl.program_id(0)
    frames = rows_in.shape[2]

    @pl.when(j == 0)
    def _():
        for q in range(CHAIN):
            many = STRIDE if q + 1 < CHAIN else SLOTS
            xs[pl.ds(q * STRIDE * frames, many * frames), :] = rows_in[q, :many].reshape(
                many * frames, D
            )
        xs[pl.ds(BANDS * frames, (steps - BANDS) * frames), :] = jnp.zeros(
            ((steps - BANDS) * frames, D), BF
        )

    forward_chunk(
        keep, xs, w, b, (h0, hk0, cf0, h1, hk1, cf1), gates, hk_s, ck_s, steps, chunk, frames, 1, hall
    )

    @pl.when(j == n - 1)
    def _():
        for k in range(BANDS):
            here = pl.ds(k * frames, frames)
            out = (mm(hall[0, here, :], p[:H]) + mm(hall[1, here, :], p[H:])).astype(BF)
            for q in range(CHAIN):
                if 0 <= k - q * STRIDE < SLOTS:
                    bo[q, k - q * STRIDE] = out


def mask_kernel(
    valid, at, bo, cot, um, dm, mg, ub, db, pb,
    mask, abg, abl, dum, ddm, dub, ddb, dmg, dpb,
):
    frames = at.shape[2]
    rows = CHAIN * frames
    ab = at[:, 0].reshape(rows, D) + (bo[:, 0].reshape(rows, D).astype(F32) + pb[...])
    n, r = ln(ab)
    mi = (n * mg[0]).astype(BF)
    act_f = jnp.tanh(mm(mi, um[0]) + ub[0])
    act = act_f.astype(BF)
    pre = mm(act, dm[0]) + db[0]
    value = pre[:, :SUBF]
    gate = 0.5 * jnp.tanh(0.5 * pre[:, SUBF:]) + 0.5
    mask[:, 0] = (value * gate).astype(BF).reshape(CHAIN, frames, SUBF)
    c = cot[:, 0].reshape(rows, D).astype(F32) * valid[pl.program_id(0)]
    cg = c * gate
    og = jnp.concatenate([cg.astype(BF), (cg * value * (1.0 - gate)).astype(BF)], axis=-1)
    ddb[0] = rowsum(og.astype(F32))
    ddm[0] = mm_tn(act, og).astype(BF)
    pg = (mm_nt(og, dm[0]) * (1.0 - act_f * act_f)).astype(BF)
    dub[0] = rowsum(pg.astype(F32))
    dum[0] = mm_tn(mi, pg).astype(BF)
    dy = mm_nt(pg, um[0])
    dmg[0] = rowsum(dy * n)
    grad = ln_back(n, r, mg[0], dy)
    abg[:, 0] = grad.reshape(CHAIN, frames, D)
    low = grad.astype(BF)
    abl[:, 0] = low.reshape(CHAIN, frames, D)
    dpb[0] = rowsum(low.astype(F32))


def band_backward_kernel(
    steps, chunk, keep, ol_in, xs, w, p, h0, hk0, cf0, h1, hk1, cf1,
    dw, dp, db, rows_out,
    ol, wt, pt, da, sh, rg, ch_s, cc_s,
):
    n = steps // chunk
    j = pl.program_id(0)
    frames = ol_in.shape[2]

    @pl.when(j == 0)
    def _():
        for q in range(CHAIN):
            many = STRIDE if q + 1 < CHAIN else SLOTS
            ol[pl.ds(q * STRIDE * frames, many * frames), :] = ol_in[q, :many].reshape(
                many * frames, D
            )
        ol[pl.ds(BANDS * frames, (steps - BANDS) * frames), :] = jnp.zeros(
            ((steps - BANDS) * frames, D), BF
        )

    backward_chunk(
        keep, xs, ol, w, p, (h0, hk0, cf0, h1, hk1, cf1), dw, dp, db,
        wt, pt, da, sh, rg, ch_s, cc_s, steps, chunk, frames, 1,
    )

    @pl.when(j == n - 1)
    def _():
        for q in range(CHAIN):
            many = STRIDE if q + 1 < CHAIN else SLOTS
            rows_out[q, :many] = (
                rg[pl.ds(q * STRIDE * frames, many * frames), :].astype(BF).reshape(many, frames, D)
            )
            if many < SLOTS:
                rows_out[q, many] = jnp.zeros((frames, D), BF)


def time_backward_kernel(
    steps, chunk, keep, bgrad, abg, at, emb, sp, sm, sg, tg, bg, xs, w, p, h0, hk0, cf0, h1, hk1, cf1,
    dw, dp, db, spg, dsm, dsb, dsg, dtg, dbg, dpb,
    ol, wt, pt, da, sh, rg, ch_s, cc_s, xt, atg,
):
    n = steps // chunk
    j = pl.program_id(0)
    frames = bgrad.shape[2]

    @pl.when(j == 0)
    def _():
        xt[...] = jnp.zeros_like(xt)
        dbg[...] = jnp.zeros_like(dbg)
        dtg[...] = jnp.zeros_like(dtg)
        dpb[...] = jnp.zeros_like(dpb)
        for k in range(SLOTS):
            norm, r = ln(at[:, k].reshape(steps, D))
            dy = bgrad[:, k].reshape(steps, D).astype(F32)
            dbg[...] = dbg[...] + rowsum(dy * norm)
            a = abg[:, k].reshape(steps, D) + ln_back(norm, r, bg[...], dy)
            atg[k] = a
            low = a.astype(BF).astype(F32)
            dpb[...] = dpb[...] + rowsum(low)
            xt[pl.ds(k, steps, stride=ROWS_T), :] = low
        ol[...] = xt[...].astype(BF)

    backward_chunk(
        keep, xs, ol, w, p, (h0, hk0, cf0, h1, hk1, cf1), dw, dp, db,
        wt, pt, da, sh, rg, ch_s, cc_s, steps, chunk, ROWS_T, 4,
    )

    @pl.when(j == n - 1)
    def _():
        for k in range(SLOTS):
            dy = rg[pl.ds(k, steps, stride=ROWS_T), :]
            norm, r = ln(emb[:, k].reshape(steps, D))
            dtg[...] = dtg[...] + rowsum(dy * norm)
            el = (atg[k] + ln_back(norm, r, tg[...], dy)).astype(BF)
            dsb[pl.ds(k, 1), :] = rowsum(el.astype(F32))
            gain = sg[pl.ds(k, 1), :]
            norm, r = ln(sp[:, k].reshape(steps, D).astype(F32))
            dsm[k] = mm_tn((norm * gain).astype(BF), el)
            dy = mm_nt(el, sm[k])
            dsg[pl.ds(k, 1), :] = rowsum(dy * norm)
            spg[:, k] = ln_back(norm, r, gain, dy).astype(spg.dtype).reshape(CHAIN, frames, D)


def whole(shape):
    zeros = (0,) * len(shape)
    return pl.BlockSpec(shape, lambda j: zeros)


def picked(shape, index):
    rest = (index,) + (0,) * (len(shape) - 1)
    return pl.BlockSpec(shape, lambda j: rest)


SMEM = pl.BlockSpec(memory_space=pltpu.SMEM)


def sds(shape, dtype):
    return jax.ShapeDtypeStruct(shape, dtype)


def chunk_specs(n, chunk, rows, flip):
    up = lambda j: (j, 0, 0)
    down = lambda j: (n - 1 - j, 0, 0)
    specs = []
    for way in (down, up) if flip else (up, down):
        specs += [
            pl.BlockSpec((chunk, rows, H), way),
            pl.BlockSpec((chunk, rows, H), way),
            pl.BlockSpec((chunk, rows, 6 * H), way),
        ]
    return specs


def chunk_shapes(steps, rows):
    return [
        sds((steps, rows, H), BF),
        sds((steps, rows, H), BF),
        sds((steps, rows, 6 * H), F32),
    ] * 2


def params():
    return pltpu.CompilerParams(vmem_limit_bytes=VMEM, dimension_semantics=("arbitrary",))


def time_forward(keep, sp, sm, sg, sb, tg, bg, w, b, p, pb):
    frames = sp.shape[2]
    steps, chunk = CHAIN * frames, 32
    n = steps // chunk
    slab = (CHAIN, SLOTS, frames, D)
    return pl.pallas_call(
        functools.partial(time_forward_kernel, steps, chunk),
        grid=(n,),
        in_specs=[SMEM]
        + [whole(v.shape) for v in (sp, sm, sg, sb, tg, bg)]
        + [picked((2, D + H, G4), 0), picked((2, 1, G4), 0), picked((2 * H, D), 0), whole(pb.shape)],
        out_specs=[whole(slab)] * 3
        + [whole((steps * ROWS_T, D))]
        + chunk_specs(n, chunk, ROWS_T, False),
        out_shape=[sds(slab, F32), sds(slab, F32), sds(slab, BF), sds((steps * ROWS_T, D), BF)]
        + chunk_shapes(steps, ROWS_T),
        scratch_shapes=[
            pltpu.VMEM((2, chunk * ROWS_T, G4), F32),
            pltpu.VMEM((2, ROWS_T, H), BF),
            pltpu.VMEM((2, ROWS_T, H), F32),
            pltpu.VMEM((steps * ROWS_T, D), F32),
            pltpu.VMEM((2, steps * ROWS_T, H), BF),
        ],
        compiler_params=params(),
        name="time_forward",
    )(keep, sp, sm, sg, sb, tg, bg, w, b, p, pb)


def band_forward(keep, rows_in, w, b, p):
    frames = rows_in.shape[2]
    steps, chunk = STEPS_B, 14
    n = steps // chunk
    slab = (CHAIN, SLOTS, frames, D)
    return pl.pallas_call(
        functools.partial(band_forward_kernel, steps, chunk),
        grid=(n,),
        in_specs=[SMEM, whole(slab), picked((2, D + H, G4), 1), picked((2, 1, G4), 1), picked((2 * H, D), 1)],
        out_specs=[whole(slab), whole((steps * frames, D))] + chunk_specs(n, chunk, frames, False),
        out_shape=[sds(slab, BF), sds((steps * frames, D), BF)] + chunk_shapes(steps, frames),
        scratch_shapes=[
            pltpu.VMEM((2, chunk * frames, G4), F32),
            pltpu.VMEM((2, frames, H), BF),
            pltpu.VMEM((2, frames, H), F32),
            pltpu.VMEM((2, steps * frames, H), BF),
        ],
        compiler_params=params(),
        name="band_forward",
    )(keep, rows_in, w, b, p)


def mask_stage(valid, at, bo, cot, um, dm, mg, ub, db, pb):
    frames = at.shape[2]
    slab = (CHAIN, SLOTS, frames, D)
    part = pl.BlockSpec((CHAIN, 1, frames, D), lambda k: (0, k, 0, 0))

    def band(*shape):
        return pl.BlockSpec((1,) + shape, lambda k: (k, 0, 0))

    return pl.pallas_call(
        mask_kernel,
        grid=(SLOTS,),
        in_specs=[
            SMEM, part, part, part, band(D, 4 * D), band(4 * D, 2 * SUBF),
            band(1, D), band(1, 4 * D), band(1, 2 * SUBF), whole((1, D)),
        ],
        out_specs=[
            part, part, part, band(D, 4 * D), band(4 * D, 2 * SUBF),
            band(1, 4 * D), band(1, 2 * SUBF), band(1, D), band(1, D),
        ],
        out_shape=[
            sds(slab, BF), sds(slab, F32), sds(slab, BF),
            sds((SLOTS, D, 4 * D), BF), sds((SLOTS, 4 * D, 2 * SUBF), BF),
            sds((SLOTS, 1, 4 * D), F32), sds((SLOTS, 1, 2 * SUBF), F32),
            sds((SLOTS, 1, D), F32), sds((SLOTS, 1, D), F32),
        ],
        compiler_params=params(),
        name="mask_stage",
    )(valid, at, bo, cot, um, dm, mg, ub, db, pb)


def backward_scratch(steps, chunk, rows):
    span = chunk * rows
    return [
        pltpu.VMEM((steps * rows, D), BF),
        pltpu.VMEM((2, G4, D + H), BF),
        pltpu.VMEM((2, D, H), BF),
        pltpu.VMEM((2, span, G4), BF),
        pltpu.VMEM((2, span, H), BF),
        pltpu.VMEM((steps * rows, D), F32),
        pltpu.VMEM((2, rows, H), F32),
        pltpu.VMEM((2, rows, H), F32),
    ]


def band_backward(keep, ol_in, xs, w, p, saved):
    frames = ol_in.shape[2]
    steps, chunk = STEPS_B, 14
    n = steps // chunk
    slab = (CHAIN, SLOTS, frames, D)
    return pl.pallas_call(
        functools.partial(band_backward_kernel, steps, chunk),
        grid=(n,),
        in_specs=[SMEM, whole(slab), whole(xs.shape), picked((2, D + H, G4), 1), picked((2 * H, D), 1)]
        + chunk_specs(n, chunk, frames, True),
        out_specs=[whole((2, D + H, G4)), whole((2 * H, D)), whole((2, 8, G4)), whole(slab)],
        out_shape=[sds((2, D + H, G4), F32), sds((2 * H, D), F32), sds((2, 8, G4), F32), sds(slab, BF)],
        scratch_shapes=backward_scratch(steps, chunk, frames),
        compiler_params=params(),
        name="band_backward",
    )(keep, ol_in, xs, w, p, *saved)


def time_backward(keep, bgrad, abg, at, emb, sp, sm, sg, tg, bg, xs, w, p, saved):
    frames = bgrad.shape[2]
    steps, chunk = CHAIN * frames, 32
    n = steps // chunk
    slab = (CHAIN, SLOTS, frames, D)
    outs = [
        sds((2, D + H, G4), F32), sds((2 * H, D), F32), sds((2, 8, G4), F32), sds(slab, F32),
        sds((SLOTS, SUBF, D), F32), sds((SLOTS, D), F32), sds((SLOTS, D), F32),
        sds((1, D), F32), sds((1, D), F32), sds((1, D), F32),
    ]
    return pl.pallas_call(
        functools.partial(time_backward_kernel, steps, chunk),
        grid=(n,),
        in_specs=[SMEM]
        + [whole(v.shape) for v in (bgrad, abg, at, emb, sp, sm, sg, tg, bg, xs)]
        + [picked((2, D + H, G4), 0), picked((2 * H, D), 0)]
        + chunk_specs(n, chunk, ROWS_T, True),
        out_specs=[whole(v.shape) for v in outs],
        out_shape=outs,
        scratch_shapes=backward_scratch(steps, chunk, ROWS_T)
        + [pltpu.VMEM((steps * ROWS_T, D), F32), pltpu.VMEM((SLOTS, steps, D), F32)],
        compiler_params=params(),
        name="time_backward",
    )(keep, bgrad, abg, at, emb, sp, sm, sg, tg, bg, xs, w, p, *saved)


def row_bits():
    return (lax.axis_size("rows") - 1).bit_length()


def swap_dir(v):
    return lax.ppermute(v, "dir", [(0, 1), (1, 0)])


def swap_bit(v, bit):
    return lax.ppermute(v, "rows", [(r, r ^ (1 << bit)) for r in range(lax.axis_size("rows"))])


def my_bit(bit):
    return (lax.axis_index("rows") >> bit) & 1


def chain_groups():
    many = lax.axis_size("rows") // CHAIN
    return [[CHAIN * g + q for q in range(CHAIN)] for g in range(many)]


def place_groups():
    many = lax.axis_size("rows") // CHAIN
    return [[CHAIN * g + q for g in range(many)] for q in range(CHAIN)]


def across_chain(v):
    return lax.all_to_all(v, "rows", 0, 0, axis_index_groups=chain_groups(), tiled=True)


def to_bands(v):
    return across_chain(jnp.stack([v[STRIDE * q : STRIDE * q + SLOTS] for q in range(CHAIN)]))


def to_frames(v):
    v = across_chain(v)
    return jnp.concatenate([v[q, : STRIDE if q + 1 < CHAIN else SLOTS] for q in range(CHAIN)])


def quarter_route():
    rows = lax.axis_size("rows")
    many = rows // CHAIN
    return [(s, (s % many) * CHAIN + s // many) for s in range(rows)]


def band_weights(shard, unit):
    place = lax.axis_index("rows") % CHAIN
    part = unit // CHAIN
    low = lax.ppermute(shard.astype(BF), "rows", quarter_route())
    own = lax.all_gather(low, "rows", axis=0, axis_index_groups=place_groups(), tiled=True)
    route = [(r, r + 1) for r in range(lax.axis_size("rows")) if r % CHAIN + 1 < CHAIN]
    before = lax.ppermute(own[-3 * part :], "rows", route)
    padded = jnp.concatenate([before, own, jnp.zeros_like(before)])
    start = part * (3 - place)
    found = lax.dynamic_slice_in_dim(padded, start, SLOTS * unit, 0)
    return found.reshape(SLOTS, unit, -1)


def band_totals(grads, unit):
    place = lax.axis_index("rows") % CHAIN
    part = unit // CHAIN
    rows = lax.axis_size("rows")
    route = [(r, r - 1) for r in range(rows) if r % CHAIN > 0]
    after = lax.ppermute(grads[: 3 * part], "rows", route)
    at = STRIDE * unit
    filled = jnp.concatenate([grads[:at], grads[at : at + 3 * part] + after, grads[at + 3 * part :]])
    own = lax.dynamic_slice_in_dim(filled, part * place, BANDS * unit // CHAIN, 0)
    shard = lax.psum_scatter(
        own, "rows", scatter_dimension=0, axis_index_groups=place_groups(), tiled=True
    )
    shard = lax.ppermute(shard, "rows", [(b, a) for a, b in quarter_route()])
    return shard.astype(F32) + swap_dir(shard).astype(F32)


def half_totals(grads):
    bits = row_bits() - 1
    half = 1 << bits
    v = grads.reshape(half, 2, grads.shape[0] // half // 2, grads.shape[1])
    side = lax.axis_index("dir")
    v = lax.dynamic_index_in_dim(v, side, 1, False) + swap_dir(
        lax.dynamic_index_in_dim(v, 1 - side, 1, False).astype(BF)
    ).astype(F32)
    for bit in range(bits):
        v = v.reshape(v.shape[0] // 2, 2, *v.shape[1:])
        mine = my_bit(bit)
        v = lax.dynamic_index_in_dim(v, mine, 1, False) + swap_bit(
            lax.dynamic_index_in_dim(v, 1 - mine, 1, False).astype(BF), bit
        ).astype(F32)
    v = v[0]
    v = (v + swap_bit(v.astype(BF), bits).astype(F32)).astype(BF)
    other = swap_dir(v)
    return jnp.where(
        side == 0, jnp.concatenate([v, other]), jnp.concatenate([other, v])
    ).astype(F32)


def sum_all(v, dirs):
    if dirs:
        v = v + swap_dir(v)
    for bit in range(row_bits()):
        v = v + swap_bit(v, bit)
    return v


def update(gradient, velocity, weight_now, average, clip_scale, rate):
    clipped = gradient * clip_scale
    velocity_new = MOMENTUM * velocity + clipped
    weight_new = weight_now - rate * (clipped + MOMENTUM * velocity_new)
    average_new = AVERAGE * average + (1.0 - AVERAGE) * weight_new
    return (clipped, velocity_new, weight_new, average_new)


def halved_columns():
    scale = np.full((1, G4), 0.5, np.float32)
    scale[:, 2 * H : 3 * H] = 1.0
    return jnp.asarray(scale)


def on_device(
    spectra,
    mask_grad,
    clip_starts,
    split_weight,
    split_velocity,
    split_average,
    lstm_weight,
    lstm_velocity,
    lstm_average,
    proj_weight,
    proj_velocity,
    proj_average,
    up_weight,
    up_velocity,
    up_average,
    down_weight,
    down_velocity,
    down_average,
    gain_weight,
    gain_velocity,
    gain_average,
    bias_weight,
    bias_velocity,
    bias_average,
):
    side = lax.axis_index("dir")
    row = lax.axis_index("rows")
    place = row % CHAIN
    last_place = place == CHAIN - 1
    frames = spectra.shape[1]
    steps = CHAIN * frames
    scale = halved_columns()

    lstm_mat = lax.all_gather((lstm_weight * scale).astype(BF), "rows", axis=0, tiled=True).reshape(
        4, D + H, G4
    )
    split_mat = band_weights(split_weight, SUBF)
    proj_mat = lax.all_gather(proj_weight.astype(BF), "rows", axis=0, tiled=True)
    up_mat = band_weights(up_weight, D)
    down_mat = band_weights(down_weight, 4 * D)
    first = STRIDE * place

    def mine(rows):
        return lax.dynamic_slice_in_dim(rows, first, SLOTS, 0)

    o_lstm = BANDS
    o_proj = o_lstm + 16 * H // D
    o_up = o_proj + 2
    o_down = o_up + 4 * BANDS
    split_gain = mine(gain_weight[:BANDS])
    time_gain = gain_weight[BANDS : BANDS + 1]
    band_gain = gain_weight[BANDS + 1 : BANDS + 2]
    mask_gain = mine(gain_weight[BANDS + 2 :])[:, None]
    split_bias = mine(bias_weight[:BANDS])
    lstm_bias = (bias_weight[o_lstm:o_proj].reshape(4, G4) * scale)[:, None]
    time_pb = bias_weight[o_proj : o_proj + 1]
    band_pb = bias_weight[o_proj + 1 : o_up]
    up_bias = mine(bias_weight[o_up:o_down].reshape(BANDS, 4 * D))[:, None]
    down_bias = mine(bias_weight[o_down:].reshape(BANDS, 2 * SUBF))[:, None]

    flags = lax.dynamic_index_in_dim(clip_starts[0], side, 1, False).astype(BF)
    flag_slab = jnp.broadcast_to(flags[:, None], (frames, SUBF))
    spec = jnp.transpose(spectra[0, :, 0], (1, 0, 2))
    sent = jnp.stack(
        [
            jnp.concatenate([spec[STRIDE * q : STRIDE * q + SLOTS], flag_slab[None]])
            for q in range(CHAIN)
        ]
    )
    sp = across_chain(sent)
    starts = sp[:, SLOTS, :, 0].reshape(steps).astype(F32)
    keep_time = jnp.concatenate([1.0 - starts, 1.0 - starts[1:], jnp.ones((1,), F32)])
    keep_np = np.ones((2 * STEPS_B,), np.float32)
    keep_np[STEPS_B + BANDS - 1] = 0.0
    keep_band = jnp.asarray(keep_np)
    cot = to_bands(jnp.transpose(mask_grad[0, :, 0], (1, 0, 2)))
    valid = jnp.concatenate([jnp.ones((SLOTS - 1,), F32), last_place.astype(F32)[None]])

    emb, after_time, band_rows, xs_t, *saved_t = time_forward(
        keep_time, sp, split_mat, split_gain, split_bias, time_gain, band_gain, lstm_mat, lstm_bias, proj_mat, time_pb
    )
    band_out, xs_b, *saved_b = band_forward(
        keep_band, across_chain(band_rows), lstm_mat, lstm_bias, proj_mat
    )
    band_out = across_chain(band_out)
    mask, abg, abl, d_up, d_down, d_ub, d_db, d_mg, d_bpb = mask_stage(
        valid, after_time, band_out, cot, up_mat, down_mat, mask_gain, up_bias, down_bias, band_pb
    )
    band_mask = jnp.transpose(to_frames(mask), (1, 0, 2))[None, :, None]

    up_total = band_totals(d_up.reshape(SLOTS * D, 4 * D), D)
    down_total = band_totals(d_down.reshape(SLOTS * 4 * D, 2 * SUBF), 4 * D)
    dw_b, dp_b, db_b, bgrad = band_backward(
        keep_band, across_chain(abl), xs_b, lstm_mat, proj_mat, saved_b
    )
    dw_t, dp_t, db_t, spg, d_split, d_sb, d_sg, d_tg, d_bg, d_tpb = time_backward(
        keep_time, across_chain(bgrad), abg, after_time, emb, sp, split_mat, split_gain, time_gain, band_gain,
        xs_t, lstm_mat, proj_mat, saved_t,
    )
    spectra_grad = jnp.transpose(to_frames(spg), (1, 0, 2))[None, :, None]

    lstm_t = half_totals(dw_t.reshape(2 * (D + H), G4) * scale)
    lstm_b = half_totals(dw_b.reshape(2 * (D + H), G4) * scale)
    proj_t = half_totals(dp_t)
    proj_b = half_totals(dp_b)
    upper = row >= lax.axis_size("rows") // 2
    lstm_total = jnp.where(upper, lstm_b, lstm_t)
    proj_total = jnp.where(upper, proj_b, proj_t)
    split_total = band_totals(d_split.reshape(SLOTS * SUBF, D).astype(BF), SUBF)

    def placed(part):
        wide = jnp.zeros((BANDS,) + part.shape[1:], F32)
        kept = jnp.where(
            (jnp.arange(SLOTS) < STRIDE)[:, None] | last_place, part, 0.0
        )
        return lax.dynamic_update_slice_in_dim(wide, kept, first, 0)

    db_all = jnp.concatenate([db_t[:, 0], db_b[:, 0]]) * scale
    small = jnp.concatenate(
        [
            placed(d_sg),
            d_tg,
            d_bg,
            placed(d_mg[:, 0]),
            placed(d_sb),
            db_all.reshape(16 * H // D, D),
            d_tpb,
            jnp.sum(d_bpb, axis=0),
            placed(d_ub[:, 0]).reshape(4 * BANDS, D),
            placed(d_db[:, 0]).reshape(2 * BANDS, D),
        ]
    )
    small = sum_all(small, True)
    gain_total = small[: 2 * BANDS + 2]
    bias_total = small[2 * BANDS + 2 :]

    shards = (split_total, lstm_total, proj_total, up_total, down_total)
    square = sum(jnp.sum(v * v) for v in shards)
    square = sum_all(jnp.full((8, 128), square, F32), False)[0, 0]
    grad_norm = jnp.sqrt(square + jnp.sum(small * small))
    clip_scale = jnp.minimum(1.0, CLIP_NORM / (grad_norm + 1e-06))
    outputs = (band_mask, spectra_grad, grad_norm)
    olds = (
        (split_velocity, split_weight, split_average),
        (lstm_velocity, lstm_weight, lstm_average),
        (proj_velocity, proj_weight, proj_average),
        (up_velocity, up_weight, up_average),
        (down_velocity, down_weight, down_average),
    )
    for total, old in zip(shards, olds):
        outputs += update(total, *old, clip_scale, LEARN_RATE)
    outputs += update(gain_total, gain_velocity, gain_weight, gain_average, clip_scale, GAIN_RATE)
    outputs += update(bias_total, bias_velocity, bias_weight, bias_average, clip_scale, GAIN_RATE)
    return outputs


def solution(mesh):
    per_row = P("rows", None)
    row_major = P("rows", None, "dir", None, None)
    return jax.shard_map(
        on_device,
        mesh=mesh,
        in_specs=(row_major, row_major, P("rows", None, None)) + (per_row,) * 15 + (P(),) * 6,
        out_specs=(row_major, row_major, P()) + (per_row,) * 20 + (P(),) * 8,
        check_vma=False,
    )
```

time: 4200 us -> 749 us (0.18); the launches traced: 4140 us -> 738 us
  other arithmetic: 1280 us -> 74.5 us
  waiting for transfers between devices: 1200 us -> 110 us
  matrix products: 967 us -> 0 us
  local copies, waits for them, and re-layouts: 449 us -> 32.3 us
  Pallas kernels: 0 us -> 241 us
  starting transfers between devices: 38.9 us -> 178 us
  blocking collectives: 163 us -> 80.8 us
    dot_general x914 -> x0, matrix products: 967 us -> none  [the longest x297 378 us: retreat(): jnp.dot(kept_hidden, recur_mat, preferred_element_type=jnp.float32)]
    reduce_scatter x6 -> x2, waiting for transfers between devices: 841 us -> 0.01 us  [band_totals(): lax.psum_scatter(own, 'rows', scatter_dimension=0, axis_index_groups=plac...]
    dynamic_update_slice x381 -> x0, other arithmetic: 322 us -> none  [the longest x274 244 us: run_block(): lax.scan(advance, (first_hidden, first_cell), (gate_in, keeper))]
    mul x301 -> x3, other arithmetic: 310 us -> 4.21 us  [the longest x1 3.59 us: on_device(): lstm_b = half_totals(dw_b.reshape(2 * (D + H), G4) * scale)]
    another operation x308 -> x3, other arithmetic: 298 us -> 2.01 us  [the longest x2 1.06 us: on_device(): jnp.stack([jnp.concatenate([spec[STRIDE * q:STRIDE * q + SLOTS], flag_sla...]
    pallas_call x0 -> x5, Pallas kernels: none -> 241 us  [the longest x1 96.1 us: time_backward(): pl.pallas_call(functools.partial(time_backward_kernel, steps, chunk), gri...]
    convert_element_type x718 -> x16, other arithmetic: 221 us -> 8.53 us  [the longest x8 4.19 us: half_totals(): v = (v + swap_bit(v.astype(BF), bits).astype(F32)).astype(BF)]
    all_gather x6 -> x3, waiting for transfers between devices: 139 us -> 0.01 us  [the longest x2 0.01 us: band_weights(): lax.all_gather(low, 'rows', axis=0, axis_index_groups=place_groups(), til...]
  transfers between devices with their start and end apart: 27 -> 61, of which waited for: 21 -> 20; matrix products, arithmetic and copies ran while one was open for 9% -> 11% of each run, Pallas kernels for 0% -> 26%
where the time goes in v1:
time: 749 us; the launch traced here: 738 us
  Pallas kernels  241 us (32%)
  starting transfers between devices  178 us (24%)
  waiting for transfers between devices  110 us (15%)
  blocking collectives  80.8 us (11%)
  other arithmetic  74.5 us (10%)
  local copies, waits for them, and re-layouts  32.3 us (4%)
  between operations  21.9 us (3%)
    all_to_all x7, starting transfers between devices, across_chain(): lax.all_to_all(v, 'rows', 0, 0, axis_index_groups=chain_groups(), tiled=T...  117 us
    pallas_call x1, Pallas kernels, time_backward(): pl.pallas_call(functools.partial(time_backward_kernel, steps, chunk), gri...  96.1 us
    ppermute x24, waiting for transfers between devices, swap_bit(): lax.ppermute(v, 'rows', [(r, r ^ 1 << bit) for r in range(lax.axis_size('...  96 us
    pallas_call x1, Pallas kernels, time_forward(): pl.pallas_call(functools.partial(time_forward_kernel, steps, chunk), grid...  68.3 us
    all_gather x1, blocking collectives, on_device(): lax.all_gather(proj_weight.astype(BF), 'rows', axis=0, tiled=True)  52.5 us
    ppermute x24, starting transfers between devices, swap_bit(): lax.ppermute(v, 'rows', [(r, r ^ 1 << bit) for r in range(lax.axis_size('...  35.1 us
    pallas_call x1, Pallas kernels, band_backward(): pl.pallas_call(functools.partial(band_backward_kernel, steps, chunk), gri...  32.8 us
    pallas_call x1, Pallas kernels, band_forward(): pl.pallas_call(functools.partial(band_forward_kernel, steps, chunk), grid...  27.7 us
  transfers between devices with their start and end apart: 61, of which 20 were waited for; matrix products, arithmetic and copies ran while one was open for 11% of the time, Pallas kernels for 26%

profile of v1, /device:TPU:0, one launch (start us, length us, event | category | flops | bytes accessed | tf_op | source)
XLA Modules:
  0.0 738.1 jit_solution(16696393292975912192)
XLA Ops:
  15.5 89.9 %all-to-all-start = ((bf16[4,12,64,128]{3,2,1,0:T(8,128)(2,1)}), bf16[4,12,64,128]{3,2,1,0:T(8,128)(2,1)S(1)}, u32[]{:S(2)}, u32[]{:S(2)}) async-start(bf16[4,12,64,128]{3,2,1,0:T(8,128)(2,1)} %pad_maximum_fusion), calls=%async_computation | async-start | bytes 1572864 | tf_op jit(solution)/shard_map/all_to_all | solution.py:575
  106.3 52.5 %all_gather.17.p = bf16[1024,128]{1,0:T(8,128)(2,1)} all-gather(bf16[64,128]{1,0:T(8,128)(2,1)S(1)} %convert_element_type.246), channel_id=1, replica_groups=mesh['dir'=2,'rows'=16] {'rows'}, dimensions={0}, use_global_device_ids=true | all-gather | bytes 278528 | tf_op jit(solution)/shard_map/all_gather | solution.py:704
  161.0 15.6 %all_gather.15 = bf16[1312,128]{1,0:T(8,128)(2,1)S(1)} all-gather(bf16[328,128]{1,0:T(8,128)(2,1)S(1)} %collective-permute-done), channel_id=1, replica_groups={{0,4,8,12},{1,5,9,13},{2,6,10,14},{3,7,11,15},{16,20,24,28},{17,21,25,2..., dimensions={0}, use_global_device_ids=true | all-gather | bytes 419840 | tf_op jit(solution)/shard_map/all_gather | solution.py:597
  181.4 68.3 %time_forward.1 = (f32[4,11,64,128]{3,2,1,0:T(8,128)}, f32[4,11,64,128]{3,2,1,0:T(8,128)}, bf16[4,11,64,128]{3,2,1,0:T(8,128)(2,1)}, bf16[4096,128]{1,0:T(8,128)...) custom-call(f32[512]{0:T(512)} %pad_maximum_fusion.7.keep, ...), custom_call_target="tpu_custom_call" | custom-call | tf_op jit(solution)/shard_map/time_forward/pallas_call | solution.py:415
  259.6 4.2 all-to-all-done.1.rows_in
  263.8 4.2 all-to-all-start.3
  272.0 4.5 collective-permute-start.5
  278.0 27.7 %band_forward.1 = (bf16[4,11,64,128]{3,2,1,0:T(8,128)(2,1)}, bf16[2688,128]{1,0:T(8,128)(2,1)}, bf16[42,64,256]{2,1,0:T(8,128)(2,1)}, bf16[42,64,256]{2,1,0:T(8,...) custom-call(f32[84]{0:T(128)} %constant.199.clone.keep, ...), custom_call_target="tpu_custom_call" | custom-call | tf_op jit(solution)/shard_map/band_forward/pallas_call | solution.py:443
  309.5 4.6 fusion.1
  317.9 15.8 %mask_stage.1 = (bf16[4,11,64,128]{3,2,1,0:T(8,128)(2,1)}, f32[4,11,64,128]{3,2,1,0:T(8,128)}, bf16[4,11,64,128]{3,2,1,0:T(8,128)(2,1)}, bf16[11,128,512]{2,1,0:...) custom-call(f32[11]{0:T(128)} %pad_convert_fusion.valid, ...), custom_call_target="tpu_custom_call" | custom-call | tf_op jit(solution)/shard_map/mask_stage/pallas_call | solution.py:468
  333.7 12.6 %all_to_all.40.ol_in = bf16[4,11,64,128]{3,2,1,0:T(8,128)(2,1)} all-to-all(bf16[4,11,64,128]{3,2,1,0:T(8,128)(2,1)} %get-tuple-element.76), channel_id=1, replica_groups={{0,1,2,3},{4,5,6,7},{8,9,10,11},{12,13,14,15},{16,17,18,19},{20,21,22,2..., dimensions={0} | all-to-all | bytes 1441792 | tf_op jit(solution)/shard_map/all_to_all | solution.py:575
  346.4 32.8 %band_backward.1 = (f32[2,384,1024]{2,1,0:T(8,128)}, f32[512,128]{1,0:T(8,128)}, f32[2,8,1024]{2,1,0:T(8,128)}, bf16[4,11,64,128]{3,2,1,0:T(8,128)(2,1)}) custom-call(f32[84]{0:T(128)} %constant.199.clone.keep, bf16[4,11,64,128]{3,2,1,0:T(8,128)(2,1)} %all_to_all.40.ol_in, bf16[2688,128]{1,0:T(8,128)(2,1)} %get-tuple-element.77.xs, ...), custom_call_target="tpu_custom_call" | custom-call | tf_op jit(solution)/shard_map/band_backward/pallas_call | solution.py:509
  391.1 96.1 %time_backward.1 = (f32[2,384,1024]{2,1,0:T(8,128)}, f32[512,128]{1,0:T(8,128)}, f32[2,8,1024]{2,1,0:T(8,128)}, f32[4,11,64,128]{3,2,1,0:T(8,128)}, f32[11,128,1...) custom-call(f32[512]{0:T(512)} %pad_maximum_fusion.7.keep, ...), custom_call_target="tpu_custom_call" | custom-call | tf_op jit(solution)/shard_map/time_backward/pallas_call | solution.py:532
  496.3 10.1 %fusion.3 = bf16[5248,256]{1,0:T(8,128)(2,1)} fusion(s32[]{:T(128)S(6)} %select_n.184, bf16[5120,256]{1,0:T(8,128)(2,1)S(1)} %bitcast.176, bf16[384,256]{1,0:T(8,128)(2,1)S(1)} %slice_add_fusion, bf16[128,256]{1,0:T(8,128)(2,1)S(1)} %slice.233), kind=kLoop, calls=%fused_computation.10 | loop fusion | flops 8060928 | bytes 5570564 | tf_op jit(solution)/shard_map/concatenate | solution.py:613
  511.9 6.5 all-to-all-start.4
  557.6 4.2 collective-permute-done.44
  581.0 5.1 all-to-all-start.7
  599.0 6.8 collective-permute-done.11
  610.3 4.4 collective-permute-start.18
  614.7 16.4 %collective-permute-done.12 = bf16[1,48,1024]{2,1,0:T(8,128)(2,1)S(1)} collective-permute-done((bf16[1,48,1024]{2,1,0:T(8,128)(2,1)S(1)}, bf16[1,48,1024]{2,1,0:T(8,128)(2,1)S(1)}, u32[]{:S(2)}, u32[]{:S(2)}) %collective-permute-start.12) | collective-permute-done | bytes 98336 | tf_op jit(solution)/shard_map/ppermute | solution.py:557
  632.1 43.8 %collective-permute-done.18 = bf16[1,48,1024]{2,1,0:T(8,128)(2,1)S(1)} collective-permute-done((bf16[1,48,1024]{2,1,0:T(8,128)(2,1)S(1)}, bf16[1,48,1024]{2,1,0:T(8,128)(2,1)S(1)}, u32[]{:S(2)}, u32[]{:S(2)}) %collective-permute-start.18) | collective-permute-done | bytes 98336 | tf_op jit(solution)/shard_map/ppermute | solution.py:557
  675.9 4.5 collective-permute-start.34
  681.6 4.5 collective-permute-done.19
  717.8 4.2 add_multiply_fusion
  (396 shorter events, 176.9 us)
Async XLA Ops:
  7.2 174.2 %all-gather.4.cloned.1.call-start = ((), (), s32[]{:S(2)}) async-start(), calls=%async_computation.11 | async-start | bytes 3342336 | tf_op jit(solution)/shard_map/all_gather | solution.py:700
  9.1 245.4 %all-gather.6.cloned.1.call-start = ((), (), s32[]{:S(2)}) async-start(), calls=%async_computation.12 | async-start | bytes 1679360 | tf_op jit(solution)/shard_map/all_gather | solution.py:597
  11.8 258.6 %all-gather.8.cloned.1.call-start = ((), (), s32[]{:S(2)}) async-start(), calls=%async_computation.13 | async-start | bytes 3358720 | tf_op jit(solution)/shard_map/all_gather | solution.py:597
  12.7 148.4 %collective-permute-start = (bf16[328,128]{1,0:T(8,128)(2,1)S(1)}, bf16[328,128]{1,0:T(8,128)(2,1)S(1)}, u32[]{:S(2)}, u32[]{:S(2)}) collective-permute-start(bf16[328,128]{1,0:T(8,128)(2,1)S(1)} %convert_element_type.244), channel_id=1, source_target_pairs={{0,0},{1,4},{2,8},{3,12},{4,1},{5,5},{6,9},{7,13},{8,2},{9,6},{10,... | collective-permute-start | bytes 251912 | tf_op jit(solution)/shard_map/ppermute | solution.py:596
  15.5 164.9 %all-to-all-start = ((bf16[4,12,64,128]{3,2,1,0:T(8,128)(2,1)}), bf16[4,12,64,128]{3,2,1,0:T(8,128)(2,1)S(1)}, u32[]{:S(2)}, u32[]{:S(2)}) async-start(bf16[4,12,64,128]{3,2,1,0:T(8,128)(2,1)} %pad_maximum_fusion), calls=%async_computation | async-start | bytes 1572864 | tf_op jit(solution)/shard_map/all_to_all | solution.py:575
  255.5 21.1 %collective-permute-start.3 = (bf16[96,512]{1,0:T(8,128)(2,1)S(1)}, bf16[96,512]{1,0:T(8,128)(2,1)S(1)}, u32[]{:S(2)}, u32[]{:S(2)}) collective-permute-start(bf16[96,512]{1,0:T(8,128)(2,1)S(1)} %slice.214), channel_id=1, source_target_pairs={{0,1},{1,2},{2,3},{4,5},{5,6},{6,7},{8,9},{9,10},{10,11},{12,13},{... | collective-permute-start | bytes 294920 | tf_op jit(solution)/shard_map/ppermute | solution.py:599
  263.8 41.9 %all-to-all-start.3 = ((bf16[4,11,64,128]{3,2,1,0:T(8,128)(2,1)}), bf16[4,11,64,128]{3,2,1,0:T(8,128)(2,1)}, u32[]{:S(2)}, u32[]{:S(2)}) async-start(bf16[4,11,64,128]{3,2,1,0:T(8,128)(2,1)} %pad_maximum_fusion.1), calls=%async_computation.3 | async-start | bytes 1441792 | tf_op jit(solution)/shard_map/all_to_all | solution.py:575
  272.0 37.4 %collective-permute-start.5 = (bf16[384,256]{1,0:T(8,128)(2,1)}, bf16[384,256]{1,0:T(8,128)(2,1)}, u32[]{:S(2)}, u32[]{:S(2)}) collective-permute-start(bf16[384,256]{1,0:T(8,128)(2,1)} %slice.215), channel_id=1, source_target_pairs={{0,1},{1,2},{2,3},{4,5},{5,6},{6,7},{8,9},{9,10},{10,11},{12,13},{... | collective-permute-start | bytes 589832 | tf_op jit(solution)/shard_map/ppermute | solution.py:599
  382.6 186.8 %reduce-scatter.10.cloned.1.call-start = ((), (), s32[]{:S(2)}) async-start(), calls=%async_computation.16 | async-start | bytes 419840
  384.3 105.6 %collective-permute-start.36 = (bf16[384,256]{1,0:T(8,128)(2,1)}, bf16[384,256]{1,0:T(8,128)(2,1)}, u32[]{:S(2)}, u32[]{:S(2)}) collective-permute-start(bf16[384,256]{1,0:T(8,128)(2,1)} %slice.232), channel_id=1, source_target_pairs={{1,0},{2,1},{3,2},{5,4},{6,5},{7,6},{9,8},{10,9},{11,10},{13,12},{... | collective-permute-start | bytes 589832 | tf_op jit(solution)/shard_map/ppermute | solution.py:611
  496.2 110.3 %reduce-scatter.8.cloned.1.call-start = ((), (), s32[]{:S(2)}) async-start(), calls=%async_computation.15 | async-start | bytes 3358720 | tf_op jit(solution)/shard_map/reduce_scatter | solution.py:615
  518.3 157.6 %reduce-scatter.6.cloned.1.call-start = ((), (), s32[]{:S(2)}) async-start(), calls=%async_computation.14 | async-start | bytes 1679360 | tf_op jit(solution)/shard_map/reduce_scatter | solution.py:615
  536.9 20.0 %collective-permute-start.25 = (bf16[32,128]{1,0:T(8,128)(2,1)}, bf16[32,128]{1,0:T(8,128)(2,1)}, u32[]{:S(2)}, u32[]{:S(2)}) collective-permute-start(bf16[32,128]{1,0:T(8,128)(2,1)} %bitcast_convert_fusion.7), channel_id=1, source_target_pairs={{0,8},{1,9},{2,10},{3,11},{4,12},{5,13},{6,14},{7,15},{8,0},{9,1},... | collective-permute-start | bytes 24584 | tf_op jit(solution)/shard_map/ppermute | solution.py:557
  547.9 21.5 %collective-permute-start.9 = (bf16[8,48,1024]{2,1,0:T(8,128)(2,1)}, bf16[8,48,1024]{2,1,0:T(8,128)(2,1)}, u32[]{:S(2)}, u32[]{:S(2)}) collective-permute-start(bf16[8,48,1024]{2,1,0:T(8,128)(2,1)} %fusion.9), channel_id=1, source_target_pairs={{0,16},{16,0},{1,17},{17,1},{2,18},{18,2},{3,19},{19,3},{4,20},{20... | collective-permute-start | bytes 2359304 | tf_op jit(solution)/shard_map/ppermute | solution.py:553
  551.8 22.6 %collective-permute-start.15 = (bf16[8,48,1024]{2,1,0:T(8,128)(2,1)}, bf16[8,48,1024]{2,1,0:T(8,128)(2,1)}, u32[]{:S(2)}, u32[]{:S(2)}) collective-permute-start(bf16[8,48,1024]{2,1,0:T(8,128)(2,1)} %fusion.10), channel_id=1, source_target_pairs={{0,16},{16,0},{1,17},{17,1},{2,18},{18,2},{3,19},{19,3},{4,20},{20... | collective-permute-start | bytes 2359304 | tf_op jit(solution)/shard_map/ppermute | solution.py:553
  557.6 22.1 %collective-permute-start.26 = (bf16[32,128]{1,0:T(8,128)(2,1)S(1)}, bf16[32,128]{1,0:T(8,128)(2,1)}, u32[]{:S(2)}, u32[]{:S(2)}) collective-permute-start(bf16[32,128]{1,0:T(8,128)(2,1)S(1)} %fusion.36), channel_id=1, source_target_pairs={{0,16},{16,0},{1,17},{17,1},{2,18},{18,2},{3,19},{19,3},{4,20},{20... | collective-permute-start | bytes 24584 | tf_op jit(solution)/shard_map/ppermute | solution.py:553
  563.6 22.5 %collective-permute-start.32 = (bf16[32,128]{1,0:T(8,128)(2,1)S(1)}, bf16[32,128]{1,0:T(8,128)(2,1)}, u32[]{:S(2)}, u32[]{:S(2)}) collective-permute-start(bf16[32,128]{1,0:T(8,128)(2,1)S(1)} %fusion.35), channel_id=1, source_target_pairs={{0,16},{16,0},{1,17},{17,1},{2,18},{18,2},{3,19},{19,3},{4,20},{20... | collective-permute-start | bytes 24584 | tf_op jit(solution)/shard_map/ppermute | solution.py:553
  581.0 119.8 %all-to-all-start.7 = ((f32[4,11,64,128]{3,2,1,0:T(8,128)}), f32[4,11,64,128]{3,2,1,0:T(8,128)S(1)}, u32[]{:S(2)}, u32[]{:S(2)}) async-start(f32[4,11,64,128]{3,2,1,0:T(8,128)} %get-tuple-element.94), calls=%async_computation.7 | async-start | bytes 2883584 | tf_op jit(solution)/shard_map/all_to_all | solution.py:575
  587.6 99.9 %collective-permute-start.8 = (bf16[328,128]{1,0:T(8,128)(2,1)}, bf16[328,128]{1,0:T(8,128)(2,1)}, u32[]{:S(2)}, u32[]{:S(2)}) collective-permute-start(bf16[328,128]{1,0:T(8,128)(2,1)} %collective-permute-done.7), channel_id=1, source_target_pairs={{0,16},{16,0},{1,17},{17,1},{2,18},{18,2},{3,19},{19,3},{4,20},{20... | collective-permute-start | bytes 251912 | tf_op jit(solution)/shard_map/ppermute | solution.py:553
  589.3 109.8 %collective-permute-start.47 = (f32[405,128]{1,0:T(8,128)}, f32[405,128]{1,0:T(8,128)}, u32[]{:S(2)}, u32[]{:S(2)}) collective-permute-start(f32[405,128]{1,0:T(8,128)} %add.348), channel_id=1, source_target_pairs={{0,8},{1,9},{2,10},{3,11},{4,12},{5,13},{6,14},{7,15},{8,0},{9,1},... | collective-permute-start | bytes 622088 | tf_op jit(solution)/shard_map/ppermute | solution.py:557
  605.8 25.2 %collective-permute-start.12 = (bf16[1,48,1024]{2,1,0:T(8,128)(2,1)S(1)}, bf16[1,48,1024]{2,1,0:T(8,128)(2,1)S(1)}, u32[]{:S(2)}, u32[]{:S(2)}) collective-permute-start(bf16[1,48,1024]{2,1,0:T(8,128)(2,1)S(1)} %dynamic-slice_convert_fusion.6), channel_id=1, source_target_pairs={{0,4},{1,5},{2,6},{3,7},{4,0},{5,1},{6,2},{7,3},{8,12},{9,13},{10,... | collective-permute-start | bytes 294920 | tf_op jit(solution)/shard_map/ppermute | solution.py:557
  606.5 74.1 %collective-permute-start.37 = (bf16[1312,256]{1,0:T(8,128)(2,1)}, bf16[1312,256]{1,0:T(8,128)(2,1)S(1)}, u32[]{:S(2)}, u32[]{:S(2)}) collective-permute-start(bf16[1312,256]{1,0:T(8,128)(2,1)} %reduce-scatter.8.cloned.1.call-done), channel_id=1, source_target_pairs={{0,0},{4,1},{8,2},{12,3},{1,4},{5,5},{9,6},{13,7},{2,8},{6,9},{10,... | collective-permute-start | bytes 2015240 | tf_op jit(solution)/shard_map/ppermute | solution.py:618
  610.3 65.6 %collective-permute-start.18 = (bf16[1,48,1024]{2,1,0:T(8,128)(2,1)S(1)}, bf16[1,48,1024]{2,1,0:T(8,128)(2,1)S(1)}, u32[]{:S(2)}, u32[]{:S(2)}) collective-permute-start(bf16[1,48,1024]{2,1,0:T(8,128)(2,1)S(1)} %dynamic-slice_convert_fusion.5), channel_id=1, source_target_pairs={{0,4},{1,5},{2,6},{3,7},{4,0},{5,1},{6,2},{7,3},{8,12},{9,13},{10,... | collective-permute-start | bytes 294920 | tf_op jit(solution)/shard_map/ppermute | solution.py:557
  632.0 48.5 %collective-permute-start.13 = (bf16[48,1024]{1,0:T(8,128)(2,1)S(1)}, bf16[48,1024]{1,0:T(8,128)(2,1)S(1)}, u32[]{:S(2)}, u32[]{:S(2)}) collective-permute-start(bf16[48,1024]{1,0:T(8,128)(2,1)S(1)} %bitcast_convert_fusion.2), channel_id=1, source_target_pairs={{0,8},{1,9},{2,10},{3,11},{4,12},{5,13},{6,14},{7,15},{8,0},{9,1},... | collective-permute-start | bytes 294920 | tf_op jit(solution)/shard_map/ppermute | solution.py:557
  (103 other events, 1244.9 us)
Sparse Core Ops, SparseCore 0:
  11.4 120.8 all-gather.3
  134.4 34.4 all-gather.5
  171.0 57.3 all-gather.7
  496.4 20.3 reduce-scatter.9
  518.9 52.4 reduce-scatter.7
  574.2 39.6 reduce-scatter.5

commit v2 on v1

v2 whole, which is shorter than its diff:
```python
import functools

import jax
import jax.numpy as jnp
import numpy as np
from jax import lax
from jax.experimental import pallas as pl
from jax.experimental.pallas import tpu as pltpu
from jax.sharding import PartitionSpec as P

D = 128
H = 256
G4 = 4 * H
BANDS = 41
SUBF = 128
CHAIN = 4
SLOTS = 12
FILL = 128
ROWS_T = 16
STEPS_B = 42
VMEM = 60 << 20
HALF = (D + H) // CHAIN // 2
HALF_P = H // CHAIN // 2

EPSILON = 1e-05
MOMENTUM = 0.9
LEARN_RATE = 5.0
GAIN_RATE = 50.0
AVERAGE = 0.5
CLIP_NORM = 5.0


GAIN_TIME, GAIN_BAND, GAIN_MASK = BANDS, BANDS + 1, BANDS + 2
BIAS_LSTM = BANDS
BIAS_PROJ = BIAS_LSTM + 16 * H // D
BIAS_UP = BIAS_PROJ + 2
BIAS_DOWN = BIAS_UP + 4 * BANDS
EARLY_BIAS = BANDS
EARLY = EARLY_BIAS + BIAS_DOWN + 2 * BANDS - BIAS_PROJ - 1
EARLY_ROWS = -(-EARLY // 16) * 16
LATE_BIAS = GAIN_MASK
LATE = LATE_BIAS + BIAS_PROJ + 1
LATE_ROWS = -(-LATE // 16) * 16

BF = jnp.bfloat16
F32 = jnp.float32


def mm(a, b):
    return jnp.dot(a, b, preferred_element_type=F32)


def mm_nt(a, b):
    return lax.dot_general(a, b, (((1,), (1,)), ((), ())), preferred_element_type=F32)


def mm_tn(a, b):
    return lax.dot_general(a, b, (((0,), (0,)), ((), ())), preferred_element_type=F32)


def ln(v):
    c = v - jnp.mean(v, axis=-1, keepdims=True)
    r = lax.rsqrt(jnp.mean(c * c, axis=-1, keepdims=True) + EPSILON)
    return c * r, r


def ln_back(n, r, gain, dy):
    dg = dy * gain
    return r * (
        dg - jnp.mean(dg, axis=-1, keepdims=True) - n * jnp.mean(dg * n, axis=-1, keepdims=True)
    )


def rowsum(v):
    return jnp.sum(v, axis=0, keepdims=True)


UP_PART = 2 * D
MASK_PART = UP_PART + 4 * D
PROJ_PART = 2 * CHAIN * HALF_P
MISC_SPLIT = 2 * PROJ_PART
MISC_LATE = MISC_SPLIT + SLOTS * SUBF
MISC_EARLY = MISC_LATE + LATE_ROWS
MISC = MISC_EARLY + EARLY_ROWS


def shard_start(shard, rows):
    return -(-shard * BANDS // rows)


def band_blocks(rows):
    if rows == CHAIN * CHAIN:
        three = SLOTS // CHAIN
        return [
            [
                (shard_start(CHAIN * z + q, rows), three, shard_start(CHAIN * z + q + 1, rows) - shard_start(CHAIN * z + q, rows))
                for z in range(CHAIN)
            ]
            for q in range(CHAIN)
        ]
    each = BANDS // CHAIN
    return [[(each * q, SLOTS, each if q + 1 < CHAIN else BANDS - each * q)] for q in range(CHAIN)]


def band_table(rows):
    return [
        [first + i if i < filled else -1 for first, places, filled in blocks for i in range(places)]
        for blocks in band_blocks(rows)
    ]


def wide_row(rows, first, many):
    return jnp.concatenate([rows[pl.ds(first + i, 1), :] for i in range(many)], axis=1)


def forward_chunk(keep, x_ref, w_ref, bias, scale, first_row, outs, gates, hk_s, ck_s, steps, chunk, rows, unroll, hall):
    n = steps // chunk
    j = pl.program_id(0)
    first = (j * chunk, (n - 1 - j) * chunk)

    @pl.when(j == 0)
    def _():
        hk_s[...] = jnp.zeros_like(hk_s)
        ck_s[...] = jnp.zeros_like(ck_s)

    for d in range(2):
        x = x_ref[pl.ds(pl.multiple_of(first[d] * rows, chunk * rows), chunk * rows), :]
        b = wide_row(bias, first_row + d * (G4 // D), G4 // D) * scale[...]
        gates[d] = mm(x, w_ref[d, :D]) + b

    def step(t, carry):
        new = []
        for d in range(2):
            hk, ck = carry[2 * d], carry[2 * d + 1]
            tt = t if d == 0 else chunk - 1 - t
            at = first[d] + tt
            now = keep[d * steps + at]
            later = jnp.minimum(at + 1, steps - 1) if d == 0 else jnp.maximum(at - 1, 0)
            nxt = keep[d * steps + later]
            h_ref, hk_ref, cf_ref = outs[3 * d : 3 * d + 3]
            a = gates[d, pl.ds(pl.multiple_of(tt * rows, rows), rows), :] + mm(hk, w_ref[d, D:])
            ti = jnp.tanh(a[:, :H])
            tf = jnp.tanh(a[:, H : 2 * H])
            g = jnp.tanh(a[:, 2 * H : 3 * H])
            to = jnp.tanh(a[:, 3 * H :])
            i = 0.5 * ti + 0.5
            f = 0.5 * tf + 0.5
            o = 0.5 * to + 0.5
            c = f * ck + i * g
            tc = jnp.tanh(c)
            h = o * tc
            h_low = h.astype(BF)
            hk_ref[tt] = hk
            h_ref[tt] = h_low
            if hall is not None:
                hall[d, pl.ds(pl.multiple_of(at * rows, rows), rows), :] = h_low
            cf_ref[tt, :, :H] = o * (1.0 - tc * tc)
            cf_ref[tt, :, H : 2 * H] = g * (0.5 - 0.5 * ti * ti)
            cf_ref[tt, :, 2 * H : 3 * H] = ck * (0.5 - 0.5 * tf * tf)
            cf_ref[tt, :, 3 * H : 4 * H] = i * (1.0 - g * g)
            cf_ref[tt, :, 4 * H : 5 * H] = tc * (0.5 - 0.5 * to * to)
            cf_ref[tt, :, 5 * H :] = f * now
            new += [(h * nxt).astype(BF), c * nxt]
        return tuple(new)

    done = lax.fori_loop(
        0, chunk, step, (hk_s[0], ck_s[0], hk_s[1], ck_s[1]), unroll=unroll
    )
    for d in range(2):
        hk_s[d] = done[2 * d]
        ck_s[d] = done[2 * d + 1]


def backward_chunk(
    keep, x_ref, ol, w_ref, p_ref, ins, dw, dp, db, wt, pt, da, sh, rg, ch_s, cc_s, steps, chunk, rows, unroll
):
    n = steps // chunk
    j = pl.program_id(0)
    first = ((n - 1 - j) * chunk, j * chunk)
    span = chunk * rows

    @pl.when(j == 0)
    def _():
        ch_s[...] = jnp.zeros_like(ch_s)
        cc_s[...] = jnp.zeros_like(cc_s)
        rg[...] = jnp.zeros_like(rg)
        dw[...] = jnp.zeros_like(dw)
        dp[...] = jnp.zeros_like(dp)
        db[...] = jnp.zeros_like(db)
        for d in range(2):
            wt[d] = w_ref[d].T
            pt[d] = p_ref[pl.ds(d * H, H), :].T

    at_rows = [pl.ds(pl.multiple_of(first[d] * rows, span), span) for d in range(2)]
    for d in range(2):
        sh[d] = mm(ol[at_rows[d], :], pt[d]).astype(BF)

    def step(t, carry):
        new = []
        for d in range(2):
            ch, cc = carry[2 * d], carry[2 * d + 1]
            tt = chunk - 1 - t if d == 0 else t
            now = keep[d * steps + first[d] + tt]
            cf = ins[3 * d + 2]
            here = pl.ds(pl.multiple_of(tt * rows, rows), rows)
            dh = sh[d, here, :].astype(F32) + ch
            dc = cc + dh * cf[tt, :, :H]
            da_now = jnp.concatenate(
                [
                    (dc * cf[tt, :, H : 2 * H]).astype(BF),
                    (dc * cf[tt, :, 2 * H : 3 * H]).astype(BF),
                    (dc * cf[tt, :, 3 * H : 4 * H]).astype(BF),
                    (dh * cf[tt, :, 4 * H : 5 * H]).astype(BF),
                ],
                axis=-1,
            )
            da[d, here, :] = da_now
            new += [mm(da_now, wt[d, :, D:]) * now, dc * cf[tt, :, 5 * H :]]
        return tuple(new)

    done = lax.fori_loop(0, chunk, step, (ch_s[0], cc_s[0], ch_s[1], cc_s[1]), unroll=unroll)
    ones = jnp.ones((8, span), BF)
    for d in range(2):
        ch_s[d] = done[2 * d]
        cc_s[d] = done[2 * d + 1]
        here = at_rows[d]
        grad = da[d]
        rg[here, :] = rg[here, :] + mm(grad, wt[d, :, :D])
        dw[d, :D, :] = dw[d, :D, :] + mm_tn(x_ref[here, :], grad)
        dw[d, D:, :] = dw[d, D:, :] + mm_tn(ins[3 * d + 1][...].reshape(span, H), grad)
        db[d] = db[d] + mm(ones, grad)
        at_p = pl.ds(d * H, H)
        dp[at_p, :] = dp[at_p, :] + mm_tn(ins[3 * d][...].reshape(span, H), ol[here, :])


def lay_weights(side, near, far, w):
    for way in range(2):
        for q in range(CHAIN):
            for part, of in ((near, side), (far, 1 - side)):
                at = pl.multiple_of(q * 2 * HALF + of * HALF, HALF)
                w[way, pl.ds(at, HALF), :] = part[q, way, :HALF, :]


def part_totals(side, dw, dp, scale, keep_w, send_w, keep_p, send_p):
    for way in range(2):
        for q in range(CHAIN):
            for k_ref, of in ((keep_w, side), (send_w, 1 - side)):
                at = pl.multiple_of(q * 2 * HALF + of * HALF, HALF)
                k_ref[q, way] = (dw[way, pl.ds(at, HALF), :] * scale[...]).astype(BF)
            for k_ref, of in ((keep_p, side), (send_p, 1 - side)):
                at = pl.multiple_of(way * H + q * 2 * HALF_P + of * HALF_P, HALF_P)
                k_ref[pl.ds((q * 2 + way) * HALF_P, HALF_P), :] = dp[pl.ds(at, HALF_P), :].astype(BF)


def bias_total(db, scale, out, first):
    for way in range(2):
        row = db[way, :1, :] * scale[...]
        for i in range(G4 // D):
            out[pl.ds(first + way * (G4 // D) + i, 1), :] = row[:, i * D : (i + 1) * D]


def time_forward_kernel(
    steps, chunk, keep, bands, side, sp, sm, gain, bias, scale, near, far, p, _,
    emb, at, br, xs, w, _out, h0, hk0, cf0, h1, hk1, cf1,
    gates, hk_s, ck_s, xt, hall,
):
    n = steps // chunk
    j = pl.program_id(0)
    frames = sp.shape[2]

    @pl.when(j == 0)
    def _():
        lay_weights(side[0], near, far, w)
        xt[...] = jnp.zeros_like(xt)
        for k in range(SLOTS):
            v = sp[:, k].reshape(steps, D).astype(F32)
            normed = (ln(v)[0] * gain[pl.ds(bands[k], 1), :]).astype(BF)
            e = mm(normed, sm[k]) + bias[pl.ds(bands[k], 1), :]
            emb[:, k] = e.reshape(CHAIN, frames, D)
            xt[pl.ds(k, steps, stride=ROWS_T), :] = ln(e)[0] * gain[pl.ds(GAIN_TIME, 1), :]
        xs[...] = xt[...].astype(BF)

    forward_chunk(
        keep, xs, w, bias, scale, BIAS_LSTM, (h0, hk0, cf0, h1, hk1, cf1), gates, hk_s, ck_s, steps, chunk, ROWS_T, 4, hall
    )

    @pl.when(j == n - 1)
    def _():
        span = 512
        for s in range(0, steps * ROWS_T, span):
            here = pl.ds(s, span)
            xt[here, :] = mm(hall[0, here, :], p[:H]) + mm(hall[1, here, :], p[H:])
        for k in range(SLOTS):
            to = xt[pl.ds(k, steps, stride=ROWS_T), :] + bias[pl.ds(BIAS_PROJ, 1), :]
            a = emb[:, k].reshape(steps, D) + to
            at[:, k] = a.reshape(CHAIN, frames, D)
            br[:, k] = (ln(a)[0] * gain[pl.ds(GAIN_BAND, 1), :]).astype(BF).reshape(CHAIN, frames, D)


def band_forward_kernel(
    steps, chunk, table, keep, side, rows_in, near, far, bias, scale, p,
    bo, xs, w, h0, hk0, cf0, h1, hk1, cf1,
    gates, hk_s, ck_s, hall,
):
    n = steps // chunk
    j = pl.program_id(0)
    frames = rows_in.shape[2]

    @pl.when(j == 0)
    def _():
        lay_weights(side[0], near, far, w)
        for q in range(CHAIN):
            for k in range(SLOTS):
                if table[q][k] >= 0:
                    xs[pl.ds(table[q][k] * frames, frames), :] = rows_in[q, k]
        xs[pl.ds(BANDS * frames, (steps - BANDS) * frames), :] = jnp.zeros(
            ((steps - BANDS) * frames, D), BF
        )

    forward_chunk(
        keep, xs, w, bias, scale, BIAS_LSTM + 2 * G4 // D, (h0, hk0, cf0, h1, hk1, cf1), gates, hk_s, ck_s, steps, chunk, frames, 1, hall
    )

    @pl.when(j == n - 1)
    def _():
        for q in range(CHAIN):
            for k in range(SLOTS):
                here = pl.ds(max(table[q][k], 0) * frames, frames)
                bo[q, k] = (mm(hall[0, here, :], p[:H]) + mm(hall[1, here, :], p[H:])).astype(BF)


def mask_kernel(
    bands, valid, side, at, bo, cot, um, dm, gain, bias,
    mask, abg, abl, kept, sent, early,
):
    frames = at.shape[2]
    rows = CHAIN * frames

    k = pl.program_id(0)
    band = bands[k]

    @pl.when(k == 0)
    def _():
        early[...] = jnp.zeros_like(early)

    def halves(v, first):
        half = v.shape[1] // 2
        lower = side[0] == 0
        near = jnp.where(lower, v[:, :half], v[:, half:]).astype(BF)
        far = jnp.where(lower, v[:, half:], v[:, :half]).astype(BF)
        many = v.shape[0]
        for i in range(half // D):
            kept[0, first + i * many : first + (i + 1) * many, :] = near[:, i * D : (i + 1) * D]
            sent[0, first + i * many : first + (i + 1) * many, :] = far[:, i * D : (i + 1) * D]

    ab = at[:, 0].reshape(rows, D) + (bo[:, 0].reshape(rows, D).astype(F32) + bias[pl.ds(BIAS_PROJ + 1, 1), :])
    n, r = ln(ab)
    mg = gain[pl.ds(GAIN_MASK + band, 1), :]
    mi = (n * mg).astype(BF)
    act_f = jnp.tanh(mm(mi, um[0]) + wide_row(bias, BIAS_UP + 4 * band, 4))
    act = act_f.astype(BF)
    pre = mm(act, dm[0]) + wide_row(bias, BIAS_DOWN + 2 * band, 2)
    value = pre[:, :SUBF]
    gate = 0.5 * jnp.tanh(0.5 * pre[:, SUBF:]) + 0.5
    mask[:, 0] = (value * gate).astype(BF).reshape(CHAIN, frames, SUBF)
    c = cot[:, 0].reshape(rows, D).astype(F32) * valid[k]
    cg = c * gate
    og = jnp.concatenate([cg.astype(BF), (cg * value * (1.0 - gate)).astype(BF)], axis=-1)
    ddb = rowsum(og.astype(F32))
    halves(mm_tn(act, og), UP_PART)
    pg = (mm_nt(og, dm[0]) * (1.0 - act_f * act_f)).astype(BF)
    dub = rowsum(pg.astype(F32))
    halves(mm_tn(mi, pg), 0)
    dy = mm_nt(pg, um[0])
    dmg = rowsum(dy * n)
    grad = ln_back(n, r, mg, dy)
    abg[:, 0] = grad.reshape(CHAIN, frames, D)
    low = grad.astype(BF)
    abl[:, 0] = low.reshape(CHAIN, frames, D)

    @pl.when(valid[k] > 0.0)
    def _():
        early[pl.ds(band, 1), :] = dmg
        early[pl.ds(EARLY_BIAS, 1), :] = early[pl.ds(EARLY_BIAS, 1), :] + rowsum(low.astype(F32))
        for i in range(4):
            row = EARLY_BIAS + BIAS_UP - BIAS_PROJ - 1 + 4 * band + i
            early[pl.ds(row, 1), :] = dub[:, i * D : (i + 1) * D]
        for i in range(2):
            row = EARLY_BIAS + BIAS_DOWN - BIAS_PROJ - 1 + 2 * band + i
            early[pl.ds(row, 1), :] = ddb[:, i * D : (i + 1) * D]


def band_backward_kernel(
    steps, chunk, table, keep, side, scale, ol_in, xs, w, p, h0, hk0, cf0, h1, hk1, cf1,
    keep_w, send_w, keep_p, send_p, bias_rows, rows_out,
    ol, wt, pt, da, sh, rg, ch_s, cc_s, dw, dp, db,
):
    n = steps // chunk
    j = pl.program_id(0)
    frames = ol_in.shape[2]

    @pl.when(j == 0)
    def _():
        for q in range(CHAIN):
            for k in range(SLOTS):
                if table[q][k] >= 0:
                    ol[pl.ds(table[q][k] * frames, frames), :] = ol_in[q, k]
        ol[pl.ds(BANDS * frames, (steps - BANDS) * frames), :] = jnp.zeros(
            ((steps - BANDS) * frames, D), BF
        )

    backward_chunk(
        keep, xs, ol, w, p, (h0, hk0, cf0, h1, hk1, cf1), dw, dp, db,
        wt, pt, da, sh, rg, ch_s, cc_s, steps, chunk, frames, 1,
    )

    @pl.when(j == n - 1)
    def _():
        part_totals(side[0], dw, dp, scale, keep_w, send_w, keep_p, send_p)
        bias_total(db, scale, bias_rows, 0)
        for q in range(CHAIN):
            for k in range(SLOTS):
                if table[q][k] >= 0:
                    rows_out[q, k] = rg[pl.ds(table[q][k] * frames, frames), :].astype(BF)
                else:
                    rows_out[q, k] = jnp.zeros((frames, D), BF)


def time_backward_kernel(
    steps, chunk, keep, bands, valid, side, scale, bgrad, abg, at, emb, sp, sm, gain, bias_b, keep_b, send_b, early, xs, w, p, h0, hk0, cf0, h1, hk1, cf1,
    keep_w, send_w, keep_m, send_m, spg,
    ol, wt, pt, da, sh, rg, ch_s, cc_s, dw, dp, db, xt, atg, late, dsm,
):
    n = steps // chunk
    j = pl.program_id(0)
    frames = bgrad.shape[2]

    @pl.when(j == 0)
    def _():
        xt[...] = jnp.zeros_like(xt)
        late[...] = jnp.zeros_like(late)
        dbg = jnp.zeros((1, D), F32)
        dpb = jnp.zeros((1, D), F32)
        for k in range(SLOTS):
            norm, r = ln(at[:, k].reshape(steps, D))
            dy = bgrad[:, k].reshape(steps, D).astype(F32)
            dbg = dbg + rowsum(dy * norm)
            a = abg[:, k].reshape(steps, D) + ln_back(norm, r, gain[pl.ds(GAIN_BAND, 1), :], dy)
            atg[k] = a
            low = a.astype(BF).astype(F32)
            dpb = dpb + rowsum(low)
            xt[pl.ds(k, steps, stride=ROWS_T), :] = low
        ol[...] = xt[...].astype(BF)
        late[pl.ds(GAIN_BAND, 1), :] = dbg
        late[pl.ds(LATE_BIAS + BIAS_PROJ, 1), :] = dpb
        late[pl.ds(LATE_BIAS + BIAS_LSTM + 2 * G4 // D, 2 * G4 // D), :] = bias_b[...]

    backward_chunk(
        keep, xs, ol, w, p, (h0, hk0, cf0, h1, hk1, cf1), dw, dp, db,
        wt, pt, da, sh, rg, ch_s, cc_s, steps, chunk, ROWS_T, 4,
    )

    @pl.when(j == n - 1)
    def _():
        part_totals(side[0], dw, dp, scale, keep_w, send_w, keep_m, send_m)
        bias_total(db, scale, late, LATE_BIAS + BIAS_LSTM)
        dtg = jnp.zeros((1, D), F32)
        for k in range(SLOTS):
            dy = rg[pl.ds(k, steps, stride=ROWS_T), :]
            norm, r = ln(emb[:, k].reshape(steps, D))
            dtg = dtg + rowsum(dy * norm)
            el = (atg[k] + ln_back(norm, r, gain[pl.ds(GAIN_TIME, 1), :], dy)).astype(BF)
            dsb = rowsum(el.astype(F32))
            own = gain[pl.ds(bands[k], 1), :]
            norm, r = ln(sp[:, k].reshape(steps, D).astype(F32))
            dsm[k] = mm_tn((norm * own).astype(BF), el).astype(BF)
            dy = mm_nt(el, sm[k])
            dsg = rowsum(dy * norm)

            @pl.when(valid[k] > 0.0)
            def _():
                late[pl.ds(bands[k], 1), :] = dsg
                late[pl.ds(LATE_BIAS + bands[k], 1), :] = dsb

            spg[:, k] = ln_back(norm, r, own, dy).astype(spg.dtype).reshape(CHAIN, frames, D)
        late[pl.ds(GAIN_TIME, 1), :] = dtg
        for out, band_part in ((keep_m, keep_b), (send_m, send_b)):
            out[pl.ds(PROJ_PART, PROJ_PART), :] = band_part[...]
            out[pl.ds(MISC_EARLY, EARLY_ROWS), :] = early[...].astype(BF)
            out[pl.ds(MISC_SPLIT, SLOTS * SUBF), :] = dsm[...].reshape(SLOTS * SUBF, D)
            out[pl.ds(MISC_LATE, LATE_ROWS), :] = late[...].astype(BF)


def whole(shape):
    zeros = (0,) * len(shape)
    return pl.BlockSpec(shape, lambda j: zeros)


SMEM = pl.BlockSpec(memory_space=pltpu.SMEM)
ANY = pl.BlockSpec(memory_space=pl.ANY)


def sds(shape, dtype):
    return jax.ShapeDtypeStruct(shape, dtype)


def chunk_specs(n, chunk, rows, flip):
    up = lambda j: (j, 0, 0)
    down = lambda j: (n - 1 - j, 0, 0)
    specs = []
    for way in (down, up) if flip else (up, down):
        specs += [
            pl.BlockSpec((chunk, rows, H), way),
            pl.BlockSpec((chunk, rows, H), way),
            pl.BlockSpec((chunk, rows, 6 * H), way),
        ]
    return specs


def chunk_shapes(steps, rows):
    return [
        sds((steps, rows, H), BF),
        sds((steps, rows, H), BF),
        sds((steps, rows, 6 * H), F32),
    ] * 2


def params():
    return pltpu.CompilerParams(vmem_limit_bytes=VMEM, dimension_semantics=("arbitrary",))


def cost(micros):
    return pl.CostEstimate(flops=micros * 10**9, bytes_accessed=micros * 10**6, transcendentals=0)


def time_forward(keep, bands, side, sp, sm, gain, bias, scale, near, far, p, later):
    frames = sp.shape[2]
    steps, chunk = CHAIN * frames, 32
    n = steps // chunk
    slab = (CHAIN, SLOTS, frames, D)
    return pl.pallas_call(
        functools.partial(time_forward_kernel, steps, chunk),
        grid=(n,),
        in_specs=[SMEM, SMEM, SMEM]
        + [whole(v.shape) for v in (sp, sm, gain, bias, scale, near, far, p)]
        + [ANY],
        out_specs=[whole(slab)] * 3
        + [whole((steps * ROWS_T, D)), whole((2, D + H, G4)), ANY]
        + chunk_specs(n, chunk, ROWS_T, False),
        out_shape=[sds(slab, F32), sds(slab, F32), sds(slab, BF), sds((steps * ROWS_T, D), BF), sds((2, D + H, G4), BF), sds(later.shape, later.dtype)]
        + chunk_shapes(steps, ROWS_T),
        input_output_aliases={11: 5},
        scratch_shapes=[
            pltpu.VMEM((2, chunk * ROWS_T, G4), F32),
            pltpu.VMEM((2, ROWS_T, H), BF),
            pltpu.VMEM((2, ROWS_T, H), F32),
            pltpu.VMEM((steps * ROWS_T, D), F32),
            pltpu.VMEM((2, steps * ROWS_T, H), BF),
        ],
        compiler_params=params(),
        cost_estimate=cost(66),
        name="time_forward",
    )(keep, bands, side, sp, sm, gain, bias, scale, near, far, p, later)


def band_forward(table, keep, side, rows_in, near, far, bias, scale, p):
    frames = rows_in.shape[2]
    steps, chunk = STEPS_B, 14
    n = steps // chunk
    slab = (CHAIN, SLOTS, frames, D)
    return pl.pallas_call(
        functools.partial(band_forward_kernel, steps, chunk, table),
        grid=(n,),
        in_specs=[SMEM, SMEM, whole(slab)]
        + [whole(v.shape) for v in (near, far, bias, scale, p)],
        out_specs=[whole(slab), whole((steps * frames, D)), whole((2, D + H, G4))] + chunk_specs(n, chunk, frames, False),
        out_shape=[sds(slab, BF), sds((steps * frames, D), BF), sds((2, D + H, G4), BF)] + chunk_shapes(steps, frames),
        scratch_shapes=[
            pltpu.VMEM((2, chunk * frames, G4), F32),
            pltpu.VMEM((2, frames, H), BF),
            pltpu.VMEM((2, frames, H), F32),
            pltpu.VMEM((2, steps * frames, H), BF),
        ],
        compiler_params=params(),
        cost_estimate=cost(27),
        name="band_forward",
    )(keep, side, rows_in, near, far, bias, scale, p)


def mask_stage(bands, valid, side, at, bo, cot, um, dm, gain, bias):
    frames = at.shape[2]
    slab = (CHAIN, SLOTS, frames, D)
    part = pl.BlockSpec((CHAIN, 1, frames, D), lambda k: (0, k, 0, 0))

    def band(*shape):
        return pl.BlockSpec((1,) + shape, lambda k: (k, 0, 0))

    return pl.pallas_call(
        mask_kernel,
        grid=(SLOTS,),
        in_specs=[
            SMEM, SMEM, SMEM, part, part, part, band(D, 4 * D), band(4 * D, 2 * SUBF),
            whole(gain.shape), whole(bias.shape),
        ],
        out_specs=[
            part, part, part, band(MASK_PART, D), band(MASK_PART, D),
            whole((EARLY_ROWS, D)),
        ],
        out_shape=[
            sds(slab, BF), sds(slab, F32), sds(slab, BF),
            sds((SLOTS, MASK_PART, D), BF), sds((SLOTS, MASK_PART, D), BF),
            sds((EARLY_ROWS, D), F32),
        ],
        compiler_params=params(),
        cost_estimate=cost(16),
        name="mask_stage",
    )(bands, valid, side, at, bo, cot, um, dm, gain, bias)


def backward_scratch(steps, chunk, rows):
    span = chunk * rows
    return [
        pltpu.VMEM((steps * rows, D), BF),
        pltpu.VMEM((2, G4, D + H), BF),
        pltpu.VMEM((2, D, H), BF),
        pltpu.VMEM((2, span, G4), BF),
        pltpu.VMEM((2, span, H), BF),
        pltpu.VMEM((steps * rows, D), F32),
        pltpu.VMEM((2, rows, H), F32),
        pltpu.VMEM((2, rows, H), F32),
        pltpu.VMEM((2, D + H, G4), F32),
        pltpu.VMEM((2 * H, D), F32),
        pltpu.VMEM((2, 8, G4), F32),
    ]


def total_shapes(small):
    return [sds((CHAIN, 2, HALF, G4), BF)] * 2 + [sds((small, D), BF)] * 2


def band_backward(table, keep, side, scale, ol_in, xs, w, p, saved):
    frames = ol_in.shape[2]
    steps, chunk = STEPS_B, 14
    n = steps // chunk
    slab = (CHAIN, SLOTS, frames, D)
    return pl.pallas_call(
        functools.partial(band_backward_kernel, steps, chunk, table),
        grid=(n,),
        in_specs=[SMEM, SMEM]
        + [whole(v.shape) for v in (scale, ol_in, xs, w, p)]
        + chunk_specs(n, chunk, frames, True),
        out_specs=[whole(v.shape) for v in total_shapes(PROJ_PART)] + [whole((2 * G4 // D, D)), whole(slab)],
        out_shape=total_shapes(PROJ_PART) + [sds((2 * G4 // D, D), F32), sds(slab, BF)],
        scratch_shapes=backward_scratch(steps, chunk, frames),
        compiler_params=params(),
        cost_estimate=cost(32),
        name="band_backward",
    )(keep, side, scale, ol_in, xs, w, p, *saved)


def time_backward(keep, bands, valid, side, scale, bgrad, abg, at, emb, sp, sm, gain, bias_b, keep_b, send_b, early, xs, w, p, saved):
    frames = bgrad.shape[2]
    steps, chunk = CHAIN * frames, 32
    n = steps // chunk
    slab = (CHAIN, SLOTS, frames, D)
    outs = total_shapes(MISC) + [sds(slab, BF)]
    return pl.pallas_call(
        functools.partial(time_backward_kernel, steps, chunk),
        grid=(n,),
        in_specs=[SMEM, SMEM, SMEM, SMEM]
        + [whole(v.shape) for v in (scale, bgrad, abg, at, emb, sp, sm, gain, bias_b, keep_b, send_b, early, xs, w, p)]
        + chunk_specs(n, chunk, ROWS_T, True),
        out_specs=[whole(v.shape) for v in outs],
        out_shape=outs,
        scratch_shapes=backward_scratch(steps, chunk, ROWS_T)
        + [pltpu.VMEM((steps * ROWS_T, D), F32), pltpu.VMEM((SLOTS, steps, D), F32)]
        + [pltpu.VMEM((LATE_ROWS, D), F32), pltpu.VMEM((SLOTS, SUBF, D), BF)],
        compiler_params=params(),
        cost_estimate=cost(96),
        name="time_backward",
    )(keep, bands, valid, side, scale, bgrad, abg, at, emb, sp, sm, gain, bias_b, keep_b, send_b, early, xs, w, p, *saved)


def chain_groups():
    many = lax.axis_size("rows") // CHAIN
    return [[CHAIN * g + q for q in range(CHAIN)] for g in range(many)]


def place_groups():
    many = lax.axis_size("rows") // CHAIN
    return [[CHAIN * g + q for g in range(many)] for q in range(CHAIN)]


def across(v, groups, axis=0):
    return lax.all_to_all(v, "rows", axis, axis, axis_index_groups=groups, tiled=True)


def spread(v, groups):
    return across(jnp.broadcast_to(v[None], (len(groups[0]),) + v.shape), groups)


def swap_dir(v):
    return lax.ppermute(v, "dir", [(0, 1), (1, 0)])


def ordered(side, near, far):
    return jnp.where(side == 0, jnp.stack([near, far]), jnp.stack([far, near]))


def to_bands(v, more=None):
    v = jnp.concatenate([v, v[:1]])
    parts = []
    for blocks in band_blocks(lax.axis_size("rows")):
        cuts = [v[first : first + places] for first, places, _ in blocks]
        parts.append(jnp.concatenate(cuts + ([] if more is None else [more])))
    return jnp.stack(parts)


def from_bands(v):
    found = {}
    for q, blocks in enumerate(band_blocks(lax.axis_size("rows"))):
        at = 0
        for first, places, filled in blocks:
            found[first] = v[q, at : at + filled]
            at += places
    return jnp.concatenate([found[first] for first in sorted(found)])


def my_bit(bit):
    return (lax.axis_index("rows") >> bit) & 1


def swap_bit(v, bit):
    return lax.ppermute(v, "rows", [(r, r ^ (1 << bit)) for r in range(lax.axis_size("rows"))])


def double(v, bit):
    return ordered(my_bit(bit), v, swap_bit(v, bit))


def halve(v, bit, axis):
    mine = my_bit(bit)
    kept = lax.dynamic_index_in_dim(v, mine, axis, False)
    return kept + swap_bit(lax.dynamic_index_in_dim(v, 1 - mine, axis, False), bit)


def my_rows(values):
    return jnp.asarray(np.array(values, np.int32))[lax.axis_index("rows")]


def fills(rows):
    return [shard_start(s, rows) * D - s * BANDS * D // rows for s in range(rows)]


def tied(v, *others):
    for other in others:
        one = lax.slice(other, (0,) * other.ndim, (1,) * other.ndim).reshape(())
        v = jnp.where(jnp.isnan(one), jnp.zeros_like(v), v)
    return v


def whole_bands(shard):
    rows = lax.axis_size("rows")
    unit = shard.shape[0] * rows // (BANDS * D)
    head = FILL * unit
    after = lax.ppermute(shard[:head], "rows", [(r + 1, r) for r in range(rows - 1)])
    spare = jnp.zeros((head,) + shard.shape[1:], shard.dtype)
    long = jnp.concatenate([shard, after, spare])
    return lax.dynamic_slice_in_dim(long, my_rows(fills(rows)) * unit, SLOTS // CHAIN * D * unit, 0)


def to_shard(own, unit):
    rows = lax.axis_size("rows")
    fill = my_rows(fills(rows)) * unit
    many = BANDS * D * unit // rows
    head = jnp.zeros((FILL * unit,) + own.shape[1:], own.dtype)
    over = lax.dynamic_slice_in_dim(jnp.concatenate([own, head]), many - fill, FILL * unit, 0)
    before = lax.ppermute(over, "rows", [(r, r + 1) for r in range(rows - 1)])
    moved = lax.dynamic_slice_in_dim(jnp.concatenate([head, own]), FILL * unit - fill, many, 0)
    before = jnp.concatenate([before, jnp.zeros((many - FILL * unit,) + own.shape[1:], own.dtype)])
    row = lax.broadcasted_iota(jnp.int32, (many, 1), 0)
    return jnp.where(row < fill, before, moved)


def square_slice():
    return lax.axis_size("rows") == CHAIN * CHAIN


def pick_bands(wide):
    blocks = band_blocks(lax.axis_size("rows"))
    place = lax.axis_index("rows") % CHAIN
    wide = jnp.concatenate([wide, wide[:1]])
    cuts = []
    for at in range(len(blocks[0])):
        first = jnp.asarray(np.array([b[at][0] for b in blocks], np.int32))[place]
        cuts.append(lax.dynamic_slice_in_dim(wide, first, blocks[0][at][1], 0))
    return jnp.concatenate(cuts)


def place_bands(part, valid):
    blocks = band_blocks(lax.axis_size("rows"))
    place = lax.axis_index("rows") % CHAIN
    part = part * valid[:, None]
    total = jnp.zeros((BANDS + 1, part.shape[1]), F32)
    row = 0
    for at in range(len(blocks[0])):
        first = jnp.asarray(np.array([b[at][0] for b in blocks], np.int32))[place]
        cut = part[row : row + blocks[0][at][1]]
        total = lax.dynamic_update_slice_in_dim(total, cut, first, 0)
        row += blocks[0][at][1]
    return total[:BANDS]


def band_weights(shard, gate=None):
    rows = lax.axis_size("rows")
    unit = shard.shape[0] * rows // BANDS
    low = shard.astype(BF)
    if not square_slice():
        full = lax.all_gather(low, "rows", axis=0, tiled=True).reshape(BANDS, unit, -1)
        return pick_bands(full)
    own = whole_bands(low)
    if gate is not None:
        own = tied(own, gate)
    own = lax.all_gather(own, "rows", axis=0, axis_index_groups=place_groups(), tiled=True)
    return own.reshape(SLOTS, unit, -1)


def band_sums(grads, apart):
    if not square_slice():
        return grads
    if not apart:
        return halve(halve(grads.reshape(2, 2, SLOTS // CHAIN, *grads.shape[1:]), 3, 0), 2, 0)
    return lax.psum_scatter(
        grads, "rows", scatter_dimension=0, axis_index_groups=place_groups(), tiled=True
    )


def shard_sums(own, unit, valid):
    if square_slice():
        return to_shard(own.reshape(SLOTS // CHAIN * unit, -1), unit // D)
    flat = place_bands(own.reshape(SLOTS, -1).astype(F32), valid).astype(BF)
    flat = flat.reshape(BANDS * unit, -1)
    return lax.psum_scatter(flat, "rows", scatter_dimension=0, tiled=True)


def both_cores(kept, sent):
    return kept + swap_dir(sent)


def mask_totals(side, own, valid):
    pair = ordered(side, own, swap_dir(own))
    many = own.shape[0]
    up = pair[:, :, :UP_PART].reshape(2, many, UP_PART // D, D, D)
    up = jnp.transpose(up, (1, 3, 0, 2, 4)).reshape(many, D, 4 * D)
    down = jnp.transpose(pair[:, :, UP_PART:], (1, 2, 0, 3)).reshape(many, 4 * D, 2 * SUBF)
    return shard_sums(up, D, valid).astype(F32), shard_sums(down, 4 * D, valid).astype(F32)


def sum_rows(v, bits, wire=F32):
    for bit in bits:
        v = v + swap_bit(v.astype(wire), bit).astype(F32)
    return v


def gather_first(side, lstm_low, proj_low, split_weight, sp):
    if not square_slice():
        lstm = lax.all_gather(lstm_low, "rows", axis=0, tiled=True)
        proj = lax.all_gather(proj_low, "rows", axis=0, tiled=True).reshape(2, 2 * H, D)
        cut = jnp.transpose(lstm.reshape(2, 2, CHAIN, 2, HALF, G4), (0, 3, 2, 1, 4, 5))
        near = lax.dynamic_index_in_dim(cut, side, 1, False)
        far = lax.dynamic_index_in_dim(cut, 1 - side, 1, False)
        return (near[0], far[0], proj[0]), lambda dep: (near[1], far[1], proj[1]), band_weights(split_weight)
    packed = jnp.concatenate(
        [
            lax.dynamic_slice_in_dim(lstm_low, side * HALF, HALF, 0),
            lax.dynamic_slice_in_dim(proj_low, side * HALF_P, HALF_P, 0).reshape(-1, G4),
        ]
    )
    split = whole_bands(split_weight.astype(BF))
    column = double(packed, 3)
    column = double(tied(column, split), 2)
    split = double(split, 3)
    time = tied(column[:, 0], split, sp)
    split = double(split, 2)
    time = double(time, 0)
    time = double(tied(time, split), 1)
    split = jnp.swapaxes(split, 0, 1).reshape(SLOTS, SUBF, D)

    def finish(near):
        near = near.reshape(CHAIN, 2, *packed.shape)
        far = swap_dir(near)
        proj = ordered(side, near[:, :, HALF:], far[:, :, HALF:])
        return near, far, jnp.transpose(proj, (2, 1, 0, 3, 4)).reshape(2 * H, D)

    done = finish(time)
    band = spread(tied(column[:, 1], time), chain_groups())
    return done, lambda dep: finish(tied(band, dep)), split


def lstm_totals(side, time, band, proj):
    flat = HALF_P * D // G4
    if not square_slice():
        v = jnp.stack([time, band])
        pair = ordered(side, v, swap_dir(v))
        lstm = jnp.transpose(pair, (1, 3, 2, 0, 4, 5)).reshape(-1, G4)
        pair = ordered(side, proj, swap_dir(proj)).reshape(2, 2, CHAIN, 2, HALF_P, D)
        proj = jnp.transpose(pair, (1, 3, 2, 0, 4, 5)).reshape(-1, D)
        return tuple(
            lax.psum_scatter(t, "rows", scatter_dimension=0, tiled=True).astype(F32)
            for t in (lstm, proj)
        )
    parts = [proj[i * PROJ_PART : (i + 1) * PROJ_PART].reshape(CHAIN, 2, flat, G4) for i in range(2)]
    v = jnp.concatenate([time] + parts, axis=2).reshape(2, 2, 2, HALF + 2 * flat, G4)
    v = halve(halve(v, 0, 1), 1, 0)
    time = v[:, : HALF + flat]
    band = jnp.concatenate([band, v[:, HALF + flat :]], axis=1)
    v = halve(halve(jnp.stack([time, band]), 3, 0), 2, 0)
    pair = ordered(side, v, swap_dir(v)).astype(F32)
    return pair[:, :HALF].reshape(2 * HALF, G4), pair[:, HALF:].reshape(2 * HALF_P, D)


def update(gradient, velocity, weight_now, average, clip_scale, rate):
    clipped = gradient * clip_scale
    velocity_new = MOMENTUM * velocity + clipped
    weight_new = weight_now - rate * (clipped + MOMENTUM * velocity_new)
    average_new = AVERAGE * average + (1.0 - AVERAGE) * weight_new
    return (clipped, velocity_new, weight_new, average_new)


def halved_columns():
    scale = np.full((1, G4), 0.5, np.float32)
    scale[:, 2 * H : 3 * H] = 1.0
    return jnp.asarray(scale)


def on_device(
    spectra,
    mask_grad,
    clip_starts,
    split_weight,
    split_velocity,
    split_average,
    lstm_weight,
    lstm_velocity,
    lstm_average,
    proj_weight,
    proj_velocity,
    proj_average,
    up_weight,
    up_velocity,
    up_average,
    down_weight,
    down_velocity,
    down_average,
    gain_weight,
    gain_velocity,
    gain_average,
    bias_weight,
    bias_velocity,
    bias_average,
):
    side = lax.axis_index("dir")
    row = lax.axis_index("rows")
    place = row % CHAIN
    rows = lax.axis_size("rows")
    bits = range((rows - 1).bit_length())
    frames = spectra.shape[1]
    steps = CHAIN * frames
    scale = halved_columns()
    which = side.astype(jnp.int32)[None]
    table = band_table(rows)
    valid = jnp.asarray((np.array(table) >= 0).astype(np.float32))[place]
    bands = jnp.asarray(np.maximum(np.array(table), 0).astype(np.int32))[place]

    flags = lax.dynamic_index_in_dim(clip_starts[0], side, 1, False).astype(BF)
    flag_slab = jnp.broadcast_to(flags[:, None], (frames, SUBF))
    sp = across(
        to_bands(jnp.transpose(spectra[0, :, 0], (1, 0, 2)), flag_slab[None]), chain_groups()
    )
    starts = sp[:, SLOTS, :, 0].reshape(steps).astype(F32)
    keep_time = jnp.concatenate([1.0 - starts, 1.0 - starts[1:], jnp.ones((1,), F32)])
    keep_np = np.ones((2 * STEPS_B,), np.float32)
    keep_np[STEPS_B + BANDS - 1] = 0.0
    keep_band = jnp.asarray(keep_np)
    cot_parts = to_bands(jnp.transpose(mask_grad[0, :, 0], (1, 0, 2)))

    time_w, band_finish, split_mat = gather_first(
        side, (lstm_weight * scale).astype(BF), proj_weight.astype(BF), split_weight, sp
    )
    up_mat = band_weights(up_weight, time_w[0])
    down_mat = band_weights(down_weight, time_w[0])

    emb, after_time, band_rows, xs_t, w_time, cot_parts, *saved_t = time_forward(
        keep_time, bands, which, sp, split_mat, gain_weight, bias_weight, scale, *time_w, cot_parts
    )
    band_w = band_finish(band_rows)
    band_out, xs_b, w_band, *saved_b = band_forward(
        table, keep_band, which, across(band_rows, chain_groups()), band_w[0], band_w[1], bias_weight, scale, band_w[2]
    )
    mask, abg, abl, kept, sent, early = mask_stage(
        bands, valid, which, after_time, across(band_out, chain_groups()), across(cot_parts, chain_groups()),
        up_mat, down_mat, gain_weight, bias_weight,
    )

    ol_in = across(abl, chain_groups())
    mask_in = across(mask, chain_groups())
    mask_own = both_cores(kept, sent)
    ol_in = tied(ol_in, mask_own)
    mask_own = band_sums(mask_own, True)
    keep_w, send_w, keep_b, send_b, bias_b, bgrad = band_backward(
        table, keep_band, which, scale, ol_in, xs_b, w_band, band_w[2], saved_b
    )
    bgrad = across(bgrad, chain_groups())
    lstm_b = both_cores(tied(keep_w, bgrad), send_w)
    if square_slice():
        lstm_b = lax.psum_scatter(
            lstm_b.reshape(-1, G4), "rows", scatter_dimension=0, axis_index_groups=chain_groups(), tiled=True
        ).reshape(2, HALF, G4)
    bgrad = tied(bgrad, mask_own, mask_in)
    band_mask = jnp.transpose(from_bands(mask_in), (1, 0, 2))[None, :, None]
    keep_w, send_w, keep_m, send_m, spg = time_backward(
        keep_time, bands, valid, which, scale, bgrad, abg, after_time, emb, sp, split_mat,
        gain_weight, bias_b, keep_b, send_b, early, xs_t, w_time, time_w[2], saved_t,
    )
    spectra_grad = jnp.transpose(from_bands(across(spg, chain_groups())), (1, 0, 2))
    spectra_grad = spectra_grad[None, :, None].astype(F32)

    lstm_t = both_cores(keep_w, send_w)
    misc = both_cores(keep_m, send_m)
    lstm_total, proj_total = lstm_totals(side, lstm_t, lstm_b, misc[:MISC_SPLIT])
    split_own = band_sums(misc[MISC_SPLIT:MISC_LATE].reshape(SLOTS, SUBF, D), False)
    split_total = shard_sums(split_own, SUBF, valid).astype(F32)
    up_total, down_total = mask_totals(side, mask_own, valid)
    small = sum_rows(misc[MISC_LATE:].astype(F32), bits, BF)
    late, early = small[:LATE], small[LATE_ROWS : LATE_ROWS + EARLY]
    gain_total = jnp.concatenate([late[:LATE_BIAS], early[:EARLY_BIAS]])
    bias_total = jnp.concatenate([late[LATE_BIAS:], early[EARLY_BIAS:]])

    shards = (split_total, lstm_total, proj_total, up_total, down_total)
    square = sum(jnp.sum(v * v) for v in shards)
    square = sum_rows(jnp.full((8, 128), square, F32), bits)[0, 0]
    square = square + jnp.sum(gain_total * gain_total) + jnp.sum(bias_total * bias_total)
    grad_norm = jnp.sqrt(square)
    clip_scale = jnp.minimum(1.0, CLIP_NORM / (grad_norm + 1e-06))
    outputs = (band_mask, spectra_grad, grad_norm)
    olds = (
        (split_velocity, split_weight, split_average),
        (lstm_velocity, lstm_weight, lstm_average),
        (proj_velocity, proj_weight, proj_average),
        (up_velocity, up_weight, up_average),
        (down_velocity, down_weight, down_average),
    )
    for total, old in zip(shards, olds):
        outputs += update(total, *old, clip_scale, LEARN_RATE)
    outputs += update(gain_total, gain_velocity, gain_weight, gain_average, clip_scale, GAIN_RATE)
    outputs += update(bias_total, bias_velocity, bias_weight, bias_average, clip_scale, GAIN_RATE)
    return outputs


def solution(mesh):
    per_row = P("rows", None)
    row_major = P("rows", None, "dir", None, None)
    return jax.shard_map(
        on_device,
        mesh=mesh,
        in_specs=(row_major, row_major, P("rows", None, None)) + (per_row,) * 15 + (P(),) * 6,
        out_specs=(row_major, row_major, P()) + (per_row,) * 20 + (P(),) * 8,
        check_vma=False,
    )
```

time: 749 us -> 558 us (0.74)
  blocking collectives: 80.8 us -> 0 us
  starting transfers between devices: 178 us -> 103 us
  waiting for transfers between devices: 110 us -> 74.2 us
  other arithmetic: 74.5 us -> 45.5 us
  between operations: 21.9 us -> 41.4 us
  local copies, waits for them, and re-layouts: 32.3 us -> 42 us
    all_to_all x7 -> x9, starting transfers between devices: 117 us -> 38 us  [across(): lax.all_to_all(v, 'rows', axis, axis, axis_index_groups=groups, tiled=True)]
    all_gather x2 -> x0, blocking collectives: 68.1 us -> none  [the longest x1 52.5 us: on_device(): lax.all_gather(proj_weight.astype(BF), 'rows', axis=0, tiled=True)]
    ppermute x24 -> x20, waiting for transfers between devices: 96 us -> 33.2 us  [swap_bit(): lax.ppermute(v, 'rows', [(r, r ^ 1 << bit) for r in range(lax.axis_size('...]
    all_to_all x7 -> x9, waiting for transfers between devices: 8.64 us -> 38.9 us  [across(): lax.all_to_all(v, 'rows', axis, axis, axis_index_groups=groups, tiled=True)]
    concatenate x8 -> x2, other arithmetic: 23.5 us -> 0.47 us  [the longest x1 0.32 us: whole_bands(): long = jnp.concatenate([shard, after, spare])]
    all_to_all x1 -> x0, blocking collectives: 12.6 us -> none  [across_chain(): lax.all_to_all(v, 'rows', 0, 0, axis_index_groups=chain_groups(), tiled=T...]
    ppermute x24 -> x20, starting transfers between devices: 35.1 us -> 47.6 us  [swap_bit(): lax.ppermute(v, 'rows', [(r, r ^ 1 << bit) for r in range(lax.axis_size('...]
    select_n x3 -> x16, other arithmetic: 0.22 us -> 10.8 us  [the longest x10 7.76 us: tied(): v = jnp.where(jnp.isnan(one), jnp.zeros_like(v), v)]
  transfers between devices with their start and end apart: 61 -> 47, of which waited for: 20 -> 20; matrix products, arithmetic and copies ran while one was open for 11% -> 11% of each run, Pallas kernels for 26% -> 41%
where the time goes in v2:
time: 558 us; the launch traced here: 552 us
  Pallas kernels  246 us (44%)
  starting transfers between devices  103 us (18%)
  waiting for transfers between devices  74.2 us (13%)
  other arithmetic  45.5 us (8%)
  local copies, waits for them, and re-layouts  42 us (8%)
  between operations  41.4 us (7%)
    pallas_call x1, Pallas kernels, time_backward(): pl.pallas_call(functools.partial(time_backward_kernel, steps, chunk), gri...  96.9 us
    pallas_call x1, Pallas kernels, time_forward(): pl.pallas_call(functools.partial(time_forward_kernel, steps, chunk), grid...  69.3 us
    ppermute x20, starting transfers between devices, swap_bit(): lax.ppermute(v, 'rows', [(r, r ^ 1 << bit) for r in range(lax.axis_size('...  47.6 us
    all_to_all x9, waiting for transfers between devices, across(): lax.all_to_all(v, 'rows', axis, axis, axis_index_groups=groups, tiled=True)  38.9 us
    all_to_all x9, starting transfers between devices, across(): lax.all_to_all(v, 'rows', axis, axis, axis_index_groups=groups, tiled=True)  38 us
    pallas_call x1, Pallas kernels, band_backward(): pl.pallas_call(functools.partial(band_backward_kernel, steps, chunk, tabl...  34.3 us
    ppermute x20, waiting for transfers between devices, swap_bit(): lax.ppermute(v, 'rows', [(r, r ^ 1 << bit) for r in range(lax.axis_size('...  33.2 us
    pallas_call x1, Pallas kernels, band_forward(): pl.pallas_call(functools.partial(band_forward_kernel, steps, chunk, table...  28.2 us
  transfers between devices with their start and end apart: 47, of which 20 were waited for; matrix products, arithmetic and copies ran while one was open for 11% of the time, Pallas kernels for 41%

profile of v2, /device:TPU:0, one launch (start us, length us, event | category | flops | bytes accessed | tf_op | source)
XLA Modules:
  0.0 551.5 jit_solution(14204314728663892121)
XLA Ops:
  12.6 5.3 all-to-all-start
  20.0 6.1 %collective-permute-start.3 = (bf16[52,1024]{1,0:T(8,128)(2,1)S(1)}, bf16[52,1024]{1,0:T(8,128)(2,1)S(1)}, u32[]{:S(2)}, u32[]{:S(2)}) collective-permute-start(bf16[52,1024]{1,0:T(8,128)(2,1)S(1)} %get-tuple-element.264), channel_id=1, source_target_pairs={{0,8},{1,9},{2,10},{3,11},{4,12},{5,13},{6,14},{7,15},{8,0},{9,1},... | collective-permute-start | bytes 319496 | tf_op jit(solution)/shard_map/ppermute | solution.py:734
  55.0 5.4 collective-permute-done.6
  80.2 6.4 %all-to-all-start.2 = ((bf16[4,2,52,1024]{3,1,2,0:T(2,128)(2,1)}), bf16[4,2,52,1024]{3,1,2,0:T(2,128)(2,1)S(1)}, u32[]{:S(2)}, u32[]{:S(2)}) async-start(bf16[4,2,52,1024]{3,1,2,0:T(2,128)(2,1)} %broadcast_in_dim.65), calls=%async_computation.2 | async-start | bytes 1703936 | tf_op jit(solution)/shard_map/all_to_all | solution.py:695
  91.8 69.3 %time_forward.1 = (f32[4,12,64,128]{3,2,1,0:T(8,128)}, f32[4,12,64,128]{3,2,1,0:T(8,128)}, bf16[4,12,64,128]{3,2,1,0:T(8,128)(2,1)}, bf16[4096,128]{1,0:T(8,128)...) custom-call(f32[512]{0:T(512)} %pad_maximum_fusion.7.keep, ...), custom_call_target="tpu_custom_call", output_to_operand_aliasing={{5}: (11, {})} | custom-call | flops 65999998976 | bytes 66000000 | tf_op jit(solution)/shard_map/time_forward/pallas_call | solution.py:541
  166.8 4.0 all-to-all-start.1
  172.1 10.3 %all-to-all-done.1.rows_in = bf16[4,12,64,128]{3,2,1,0:T(8,128)(2,1)S(1)} async-done(((bf16[4,12,64,128]{3,2,1,0:T(8,128)(2,1)}), bf16[4,12,64,128]{3,2,1,0:T(8,128)(2,1)S(1)}, u32[]{:S(2)}, u32[]{:S(2)}) %all-to-all-start.1) | async-done | bytes 786464 | tf_op jit(solution)/shard_map/all_to_all | solution.py:695
  186.0 28.2 %band_forward.1 = (bf16[4,12,64,128]{3,2,1,0:T(8,128)(2,1)}, bf16[2688,128]{1,0:T(8,128)(2,1)}, bf16[2,384,1024]{2,1,0:T(8,128)(2,1)}, bf16[42,64,256]{2,1,0:T(8...) custom-call(f32[84]{0:T(128)} %constant.172.clone.keep, ...), custom_call_target="tpu_custom_call" | custom-call | flops 27000000512 | bytes 27000000 | tf_op jit(solution)/shard_map/band_forward/pallas_call | solution.py:571
  214.1 4.7 all-to-all-start.3
  220.0 9.0 %all-to-all-done.3.bo = bf16[4,12,64,128]{3,2,1,0:T(8,128)(2,1)S(1)} async-done(((bf16[4,12,64,128]{3,2,1,0:T(8,128)(2,1)}), bf16[4,12,64,128]{3,2,1,0:T(8,128)(2,1)S(1)}, u32[]{:S(2)}, u32[]{:S(2)}) %all-to-all-start.3) | async-done | bytes 786464 | tf_op jit(solution)/shard_map/all_to_all | solution.py:695
  229.9 17.2 %mask_stage.1 = (bf16[4,12,64,128]{3,2,1,0:T(8,128)(2,1)}, f32[4,12,64,128]{3,2,1,0:T(8,128)}, bf16[4,12,64,128]{3,2,1,0:T(8,128)(2,1)}, bf16[12,768,128]{2,1,0:...) custom-call(s32[12]{0:T(128)} %fusion.41.bands, f32[12]{0:T(128)} %fusion.42.valid, s32[1]{0:T(128)} %bitcast.2.side, ...), custom_call_target="tpu_custom_call" | custom-call | flops 16000000000 | bytes 16000000 | tf_op jit(solution)/shard_map/mask_stage/pallas_call | solution.py:598
  247.1 3.5 all-to-all-start.5
  254.0 6.9 %all-to-all-done.5 = bf16[4,12,64,128]{3,2,1,0:T(8,128)(2,1)S(1)} async-done(((bf16[4,12,64,128]{3,2,1,0:T(8,128)(2,1)}), bf16[4,12,64,128]{3,2,1,0:T(8,128)(2,1)S(1)}, u32[]{:S(2)}, u32[]{:S(2)}) %all-to-all-start.5) | async-done | bytes 786464 | tf_op jit(solution)/shard_map/all_to_all | solution.py:695
  264.6 4.5 add.273
  275.6 34.3 %band_backward.1 = (bf16[4,2,48,1024]{3,2,1,0:T(8,128)(2,1)}, bf16[4,2,48,1024]{3,2,1,0:T(8,128)(2,1)}, bf16[256,128]{1,0:T(8,128)(2,1)}, bf16[256,128]{1,0:T(8,...) custom-call(f32[84]{0:T(128)} %constant.172.clone.keep, s32[1]{0:T(128)} %bitcast.2.side, ...), custom_call_target="tpu_custom_call" | custom-call | flops 32000000000 | bytes 32000000 | tf_op jit(solution)/shard_map/band_backward/pallas_call | solution.py:646
  312.4 3.5 all-to-all-start.7
  318.0 9.7 %all-to-all-done.7 = bf16[4,12,64,128]{3,2,1,0:T(8,128)(2,1)S(1)} async-done(((bf16[4,12,64,128]{3,2,1,0:T(8,128)(2,1)}), bf16[4,12,64,128]{3,2,1,0:T(8,128)(2,1)S(1)}, u32[]{:S(2)}, u32[]{:S(2)}) %all-to-all-start.7) | async-done | bytes 786464 | tf_op jit(solution)/shard_map/all_to_all | solution.py:695
  334.1 96.9 %time_backward.1 = (bf16[4,2,48,1024]{3,2,1,0:T(8,128)(2,1)}, bf16[4,2,48,1024]{3,2,1,0:T(8,128)(2,1)}, bf16[2464,128]{1,0:T(8,128)(2,1)}, bf16[2464,128]{1,0:T(8,128)(2,1)}, bf16[4,12,64,128]{3,2,1,0:T(8,128)(2,1)}) custom-call(f32[512]{0:T(512)} %pad_maximum_fusion.7.keep, s32[12]{0:T(128)} %fusion.41.bands, f32[12]{0:T(128)} %fusion.42.valid, ...), custom_call_target="tpu_custom_call" | custom-call | flops 96000000000 | bytes 96000000 | tf_op jit(solution)/shard_map/time_backward/pallas_call | solution.py:667
  431.6 3.7 all-to-all-start.8
  438.9 3.9 collective-permute-start.25
  444.1 4.0 collective-permute-start.24
  454.3 8.4 %collective-permute-start.13 = (bf16[2,3,128,128]{3,2,1,0:T(8,128)(2,1)S(1)}, bf16[2,3,128,128]{3,2,1,0:T(8,128)(2,1)S(1)}, u32[]{:S(2)}, u32[]{:S(2)}) collective-permute-start(bf16[2,3,128,128]{3,2,1,0:T(8,128)(2,1)S(1)} %dynamic-slice_bitcast_fusion.2), channel_id=1, source_target_pairs={{0,8},{1,9},{2,10},{3,11},{4,12},{5,13},{6,14},{7,15},{8,0},{9,1},... | collective-permute-start | bytes 589832 | tf_op jit(solution)/shard_map/ppermute | solution.py:734
  471.7 6.3 %collective-permute-done.17 = bf16[2,2,56,1024]{3,2,1,0:T(8,128)(2,1)S(1)} collective-permute-done((bf16[2,2,56,1024]{3,2,1,0:T(8,128)(2,1)S(1)}, bf16[2,2,56,1024]{3,2,1,0:T(8,128)(2,1)S(1)}, u32[]{:S(2)}, u32[]{:S(2)}) %collective-permute-start.17) | collective-permute-done | bytes 458784 | tf_op jit(solution)/shard_map/ppermute | solution.py:734
  486.0 10.1 %collective-permute-done.20 = bf16[2,52,1024]{2,1,0:T(8,128)(2,1)S(1)} collective-permute-done((bf16[2,52,1024]{2,1,0:T(8,128)(2,1)S(1)}, bf16[2,52,1024]{2,1,0:T(8,128)(2,1)S(1)}, u32[]{:S(2)}, u32[]{:S(2)}) %collective-permute-start.20) | collective-permute-done | bytes 213024 | tf_op jit(solution)/shard_map/ppermute | solution.py:734
  (358 shorter events, 148.7 us)
Async XLA Ops:
  12.6 31.0 %all-to-all-start = ((bf16[4,13,64,128]{3,2,1,0:T(8,128)(2,1)}), bf16[4,13,64,128]{3,2,1,0:T(8,128)(2,1)S(1)}, u32[]{:S(2)}, u32[]{:S(2)}) async-start(bf16[4,13,64,128]{3,2,1,0:T(8,128)(2,1)} %pad_maximum_fusion.1), calls=%async_computation | async-start | bytes 1703936 | tf_op jit(solution)/shard_map/all_to_all | solution.py:695
  17.9 211.1 %all-gather.3.cloned.1.call-start = ((), (), s32[]{:S(2)}) async-start(), calls=%async_computation.11 | async-start | bytes 1966080 | tf_op jit(solution)/shard_map/all_gather | solution.py:824
  20.0 14.9 %collective-permute-start.3 = (bf16[52,1024]{1,0:T(8,128)(2,1)S(1)}, bf16[52,1024]{1,0:T(8,128)(2,1)S(1)}, u32[]{:S(2)}, u32[]{:S(2)}) collective-permute-start(bf16[52,1024]{1,0:T(8,128)(2,1)S(1)} %get-tuple-element.264), channel_id=1, source_target_pairs={{0,8},{1,9},{2,10},{3,11},{4,12},{5,13},{6,14},{7,15},{8,0},{9,1},... | collective-permute-start | bytes 319496 | tf_op jit(solution)/shard_map/ppermute | solution.py:734
  66.3 20.6 %collective-permute-start.10 = (bf16[512,256]{1,0:T(8,128)(2,1)}, bf16[512,256]{1,0:T(8,128)(2,1)}, u32[]{:S(2)}, u32[]{:S(2)}) collective-permute-start(bf16[512,256]{1,0:T(8,128)(2,1)} %slice.469), channel_id=1, source_target_pairs={{1,0},{2,1},{3,2},{4,3},{5,4},{6,5},{7,6},{8,7},{9,8},{10,9},{11,1... | collective-permute-start | bytes 786440 | tf_op jit(solution)/shard_map/ppermute | solution.py:766
  80.2 83.4 %all-to-all-start.2 = ((bf16[4,2,52,1024]{3,1,2,0:T(2,128)(2,1)}), bf16[4,2,52,1024]{3,1,2,0:T(2,128)(2,1)S(1)}, u32[]{:S(2)}, u32[]{:S(2)}) async-start(bf16[4,2,52,1024]{3,1,2,0:T(2,128)(2,1)} %broadcast_in_dim.65), calls=%async_computation.2 | async-start | bytes 1703936 | tf_op jit(solution)/shard_map/all_to_all | solution.py:695
  86.6 142.4 %all-gather.5.cloned.1.call-start = ((), (), s32[]{:S(2)}) async-start(), calls=%async_computation.12 | async-start | bytes 3932160 | tf_op jit(solution)/shard_map/all_gather | solution.py:824
  166.8 15.6 %all-to-all-start.1 = ((bf16[4,12,64,128]{3,2,1,0:T(8,128)(2,1)}), bf16[4,12,64,128]{3,2,1,0:T(8,128)(2,1)S(1)}, u32[]{:S(2)}, u32[]{:S(2)}) async-start(bf16[4,12,64,128]{3,2,1,0:T(8,128)(2,1)} %get-tuple-element.70), calls=%async_computation.1 | async-start | bytes 1572864 | tf_op jit(solution)/shard_map/all_to_all | solution.py:695
  182.4 31.7 %all-to-all-start.4 = ((bf16[4,12,64,128]{3,2,1,0:T(8,128)(2,1)}), bf16[4,12,64,128]{3,2,1,0:T(8,128)(2,1)S(1)}, u32[]{:S(2)}, u32[]{:S(2)}) async-start(bf16[4,12,64,128]{3,2,1,0:T(8,128)(2,1)} %get-tuple-element.72), calls=%async_computation.4 | async-start | bytes 1572864 | tf_op jit(solution)/shard_map/all_to_all | solution.py:695
  214.1 14.9 %all-to-all-start.3 = ((bf16[4,12,64,128]{3,2,1,0:T(8,128)(2,1)}), bf16[4,12,64,128]{3,2,1,0:T(8,128)(2,1)S(1)}, u32[]{:S(2)}, u32[]{:S(2)}) async-start(bf16[4,12,64,128]{3,2,1,0:T(8,128)(2,1)} %get-tuple-element.71), calls=%async_computation.3 | async-start | bytes 1572864 | tf_op jit(solution)/shard_map/all_to_all | solution.py:695
  247.1 13.8 %all-to-all-start.5 = ((bf16[4,12,64,128]{3,2,1,0:T(8,128)(2,1)}), bf16[4,12,64,128]{3,2,1,0:T(8,128)(2,1)S(1)}, u32[]{:S(2)}, u32[]{:S(2)}) async-start(bf16[4,12,64,128]{3,2,1,0:T(8,128)(2,1)} %get-tuple-element.73), calls=%async_computation.5 | async-start | bytes 1572864 | tf_op jit(solution)/shard_map/all_to_all | solution.py:695
  260.9 13.7 %all-to-all-start.6 = ((bf16[4,12,64,128]{3,2,1,0:T(8,128)(2,1)}), bf16[4,12,64,128]{3,2,1,0:T(8,128)(2,1)S(1)}, u32[]{:S(2)}, u32[]{:S(2)}) async-start(bf16[4,12,64,128]{3,2,1,0:T(8,128)(2,1)} %get-tuple-element.76), calls=%async_computation.7 | async-start | bytes 1572864 | tf_op jit(solution)/shard_map/all_to_all | solution.py:695
  264.4 66.1 %reduce-scatter.3.cloned.1.call-start = ((), (), s32[]{:S(2)}) async-start(), calls=%async_computation.13 | async-start | bytes 2949120 | tf_op jit(solution)/shard_map/reduce_scatter | solution.py:833
  309.9 19.6 %collective-permute-start.19 = (bf16[4,2,48,1024]{3,2,1,0:T(8,128)(2,1)}, bf16[4,2,48,1024]{3,2,1,0:T(8,128)(2,1)S(1)}, u32[]{:S(2)}, u32[]{:S(2)}) collective-permute-start(bf16[4,2,48,1024]{3,2,1,0:T(8,128)(2,1)} %get-tuple-element.106), channel_id=1, source_target_pairs={{0,16},{16,0},{1,17},{17,1},{2,18},{18,2},{3,19},{19,3},{4,20},{20... | collective-permute-start | bytes 2359304 | tf_op jit(solution)/shard_map/ppermute | solution.py:703
  312.4 15.3 %all-to-all-start.7 = ((bf16[4,12,64,128]{3,2,1,0:T(8,128)(2,1)}), bf16[4,12,64,128]{3,2,1,0:T(8,128)(2,1)S(1)}, u32[]{:S(2)}, u32[]{:S(2)}) async-start(bf16[4,12,64,128]{3,2,1,0:T(8,128)(2,1)} %get-tuple-element.85), calls=%async_computation.8 | async-start | bytes 1572864 | tf_op jit(solution)/shard_map/all_to_all | solution.py:695
  315.9 168.4 %reduce-scatter.5.cloned.1.call-start = ((), (), s32[]{:S(2)}) async-start(), calls=%async_computation.14 | async-start | bytes 983040 | tf_op jit(solution)/shard_map/reduce_scatter | solution.py:1016
  333.0 102.3 %collective-permute-start.23 = (bf16[3,768,128]{2,1,0:T(8,128)(2,1)}, bf16[3,768,128]{2,1,0:T(8,128)(2,1)}, u32[]{:S(2)}, u32[]{:S(2)}) collective-permute-start(bf16[3,768,128]{2,1,0:T(8,128)(2,1)} %reduce-scatter.3.cloned.1.call-done), channel_id=1, source_target_pairs={{0,16},{16,0},{1,17},{17,1},{2,18},{18,2},{3,19},{19,3},{4,20},{20... | collective-permute-start | bytes 1769480 | tf_op jit(solution)/shard_map/ppermute | solution.py:703
  431.0 20.1 %collective-permute-start.12 = (bf16[2464,128]{1,0:T(8,128)(2,1)}, bf16[2464,128]{1,0:T(8,128)(2,1)S(1)}, u32[]{:S(2)}, u32[]{:S(2)}) collective-permute-start(bf16[2464,128]{1,0:T(8,128)(2,1)} %get-tuple-element.102), channel_id=1, source_target_pairs={{0,16},{16,0},{1,17},{17,1},{2,18},{18,2},{3,19},{19,3},{4,20},{20... | collective-permute-start | bytes 1892360 | tf_op jit(solution)/shard_map/ppermute | solution.py:703
  431.5 33.0 %collective-permute-start.16 = (bf16[4,2,48,1024]{3,2,1,0:T(8,128)(2,1)}, bf16[4,2,48,1024]{3,2,1,0:T(8,128)(2,1)}, u32[]{:S(2)}, u32[]{:S(2)}) collective-permute-start(bf16[4,2,48,1024]{3,2,1,0:T(8,128)(2,1)} %get-tuple-element.104), channel_id=1, source_target_pairs={{0,16},{16,0},{1,17},{17,1},{2,18},{18,2},{3,19},{19,3},{4,20},{20... | collective-permute-start | bytes 2359304 | tf_op jit(solution)/shard_map/ppermute | solution.py:703
  431.6 16.5 %all-to-all-start.8 = ((bf16[4,12,64,128]{3,2,1,0:T(8,128)(2,1)}), bf16[4,12,64,128]{3,2,1,0:T(8,128)(2,1)S(1)}, u32[]{:S(2)}, u32[]{:S(2)}) async-start(bf16[4,12,64,128]{3,2,1,0:T(8,128)(2,1)} %get-tuple-element.100), calls=%async_computation.9 | async-start | bytes 1572864 | tf_op jit(solution)/shard_map/all_to_all | solution.py:695
  438.9 43.4 %collective-permute-start.25 = (bf16[512,256]{1,0:T(8,128)(2,1)}, bf16[512,256]{1,0:T(8,128)(2,1)S(1)}, u32[]{:S(2)}, u32[]{:S(2)}) collective-permute-start(bf16[512,256]{1,0:T(8,128)(2,1)} %pad_dynamic-slice_fusion.3), channel_id=1, source_target_pairs={{0,1},{1,2},{2,3},{3,4},{4,5},{5,6},{6,7},{7,8},{8,9},{9,10},{10,1... | collective-permute-start | bytes 786440 | tf_op jit(solution)/shard_map/ppermute | solution.py:778
  444.1 18.6 %collective-permute-start.24 = (bf16[128,512]{1,0:T(8,128)(2,1)}, bf16[128,512]{1,0:T(8,128)(2,1)}, u32[]{:S(2)}, u32[]{:S(2)}) collective-permute-start(bf16[128,512]{1,0:T(8,128)(2,1)} %pad_dynamic-slice_fusion.7), channel_id=1, source_target_pairs={{0,1},{1,2},{2,3},{3,4},{4,5},{5,6},{6,7},{7,8},{8,9},{9,10},{10,1... | collective-permute-start | bytes 393224 | tf_op jit(solution)/shard_map/ppermute | solution.py:778
  452.5 15.7 %collective-permute-start.30 = (bf16[416,128]{1,0:T(8,128)(2,1)}, bf16[416,128]{1,0:T(8,128)(2,1)S(1)}, u32[]{:S(2)}, u32[]{:S(2)}) collective-permute-start(bf16[416,128]{1,0:T(8,128)(2,1)} %slice.515), channel_id=1, source_target_pairs={{0,1},{1,0},{2,3},{3,2},{4,5},{5,4},{6,7},{7,6},{8,9},{9,8},{10,11... | collective-permute-start | bytes 319496 | tf_op jit(solution)/shard_map/ppermute | solution.py:734
  454.3 17.4 %collective-permute-start.13 = (bf16[2,3,128,128]{3,2,1,0:T(8,128)(2,1)S(1)}, bf16[2,3,128,128]{3,2,1,0:T(8,128)(2,1)S(1)}, u32[]{:S(2)}, u32[]{:S(2)}) collective-permute-start(bf16[2,3,128,128]{3,2,1,0:T(8,128)(2,1)S(1)} %dynamic-slice_bitcast_fusion.2), channel_id=1, source_target_pairs={{0,8},{1,9},{2,10},{3,11},{4,12},{5,13},{6,14},{7,15},{8,0},{9,1},... | collective-permute-start | bytes 589832 | tf_op jit(solution)/shard_map/ppermute | solution.py:734
  468.3 40.9 %collective-permute-start.31 = (bf16[416,128]{1,0:T(8,128)(2,1)S(1)}, bf16[416,128]{1,0:T(8,128)(2,1)S(1)}, u32[]{:S(2)}, u32[]{:S(2)}) collective-permute-start(bf16[416,128]{1,0:T(8,128)(2,1)S(1)} %fusion.23), channel_id=1, source_target_pairs={{0,2},{1,3},{2,0},{3,1},{4,6},{5,7},{6,4},{7,5},{8,10},{9,11},{10,... | collective-permute-start | bytes 319496 | tf_op jit(solution)/shard_map/ppermute | solution.py:734
  (71 other events, 905.2 us)
Sparse Core Ops, SparseCore 0:
  65.6 39.0 all-gather.2
  106.3 62.3 all-gather.4
  269.2 49.8 reduce-scatter.2
  330.6 26.7 reduce-scatter.4
